TPU v7x, 128 devices: a whole 4x4x4 slice. The times are simulated.
128 devices in a mesh: section: 2 (over core), dp: 16 (over x, y), tensor: 4 (over z).
Axes of the slice: x: 4, y: 4, z: 4, core: 2. Of those that a mesh axis runs over, the one named last changes fastest.
Arguments:
- tokens: bfloat16 [4096, 768], P('dp'), may hold values from -6 to 6
- cotangent: bfloat16 [4096, 768], P('dp'), may hold values from -6 to 6
- norm_gains: bfloat16 [2, 2, 768], P('section'), may hold values from 0.5 to 1.5
- w_qkv: bfloat16 [2, 3, 768, 768], P('section', None, None, 'tensor'), may hold values from -0.21875 to 0.21875
- w_attn_out: bfloat16 [2, 768, 768], P('section', 'tensor'), may hold values from -0.875 to 0.875
- bias_table: bfloat16 [2, 16, 12], P('section', None, 'tensor'), may hold values from -4 to 4
- router: bfloat16 [2, 768, 32], P('section'), may hold values from -0.15625 to 0.15625
- w_in: bfloat16 [2, 32, 768, 3072], P('section', 'dp', None, 'tensor'), may hold values from -0.21875 to 0.21875
- w_out: bfloat16 [2, 32, 3072, 768], P('section', 'dp', 'tensor'), may hold values from -0.21875 to 0.21875
- routes: int32 [2, 4096, 2], P('section', 'dp'), may hold values from 0 to 31, all different within a row; in each aligned block of 128 rows (0 to 127, 128 to 255, ..., all dimensions but the last counted through in order) at most 12 rows name the same one
- segments: int32 [32, 128], P('dp'), may hold values from 0 to 3, never falling along the last dimension, each value on 1 to 64 neighbouring positions
Outputs:
- activations: bfloat16 [2, 4096, 768], P('section', 'dp')
- input_grads: float32 [2, 4096, 768], P('section', 'dp')
- gain_grads: float32 [2, 2, 768], P('section')
- qkv_grads: float32 [2, 3, 768, 768], P('section', None, None, 'tensor')
- attn_out_grads: float32 [2, 768, 768], P('section', 'tensor')
- bias_grads: float32 [2, 16, 12], P('section', None, 'tensor')
- router_grads: float32 [2, 768, 32], P('section')
- w_in_grads: float32 [2, 32, 768, 3072], P('section', 'dp', None, 'tensor')
- w_out_grads: float32 [2, 32, 3072, 768], P('section', 'dp', 'tensor')
Inputs may be any that keep to these rules, and one draw needn't show every extreme that they name: `routes`: within each aligned block of 128 rows of one layer (one micro-batch of one data group), no expert is named by more than 12 rows, and in some block an expert is named by exactly 12; a row names two different experts. `segments`: along a row the sequence numbers never fall; each sequence spans 1 to 64 positions, and one spans exactly that many.
All inputs are finite; a program needn't handle non-finite values.
Results may differ from a plain program's by a relative error of at most 0.04.
Values may be sent and summed in bfloat16 or wider, within the bound.
A program may use at most 128 MiB of HBM per device.

v0:
```python
import jax
import jax.numpy as jnp
from jax import lax
from jax.sharding import PartitionSpec as P

epsilon = 1e-06
masked_score = -1000000000.0
bucket_edges = (1, 2, 3, 4, 5, 6, 7, 8, 10, 13, 16, 20, 25, 32, 40)


def from_behind(value, axis, steps):
    count = lax.axis_size(axis)
    leading, last = (max(0, -steps), min(count, count - steps))
    return lax.ppermute(value, axis, [(source, source + steps) for source in range(leading, last)])


def rms_scale(values):
    return lax.rsqrt(jnp.mean(values * values, axis=-1, keepdims=True) + epsilon)


def norm_gradient_return(values, inv_rms, gain_row, grad_out):
    normed = values * inv_rms
    grad_normed = grad_out * gain_row
    grad_values = inv_rms * (
        grad_normed - normed * jnp.mean(grad_normed * normed, axis=-1, keepdims=True)
    )
    return (grad_values, jnp.sum(grad_out * normed, axis=0))


def score_layout(segment_row):
    row_count = segment_row.shape[0]
    position = lax.broadcasted_iota(jnp.int32, (row_count, row_count), 0)
    other_pos = lax.broadcasted_iota(jnp.int32, (row_count, row_count), 1)
    allowed = (position >= other_pos) & (segment_row[:, None] == segment_row[None, :])
    distance = jnp.maximum(position - other_pos, 0)
    bucket = jnp.sum(
        (distance[:, :, None] >= jnp.asarray(bucket_edges, jnp.int32)).astype(jnp.int32), axis=-1
    )
    bucket_ids = jnp.arange(len(bucket_edges) + 1, dtype=jnp.int32)
    bucket_onehot_mask = (bucket_ids[:, None, None] == bucket[None, :, :]).astype(jnp.bfloat16)
    return (allowed, bucket_onehot_mask)


def heads_total(partial_value):
    return lax.psum(partial_value.astype(jnp.bfloat16), "tensor").astype(jnp.float32)


def dispatch(buffer):
    return lax.all_to_all(buffer, "dp", split_axis=0, concat_axis=0, tiled=True)


def settle(partial_value):
    summed = lax.psum(partial_value, "tensor").astype(jnp.bfloat16)
    return lax.all_to_all(summed, "dp", split_axis=0, concat_axis=0, tiled=True)


def route_slots(route_pairs, experts, capacity):
    expert_ids = route_pairs.reshape(-1)
    expert_hits = (expert_ids[:, None] == jnp.arange(experts, dtype=jnp.int32)[None, :]).astype(
        jnp.bfloat16
    )
    assignments = expert_ids.shape[0]
    earlier = (
        lax.broadcasted_iota(jnp.int32, (assignments, assignments), 0)
        > lax.broadcasted_iota(jnp.int32, (assignments, assignments), 1)
    ).astype(jnp.bfloat16)
    before = jnp.dot(earlier, expert_hits, preferred_element_type=jnp.float32)
    slot_rank = jnp.sum(before * expert_hits.astype(jnp.float32), axis=1).astype(jnp.int32)
    return expert_ids * capacity + slot_rank


def attend_scores(heads_view, position_bias_rows, allowed, bucket_onehot_mask):
    head_size = heads_view.shape[3]
    scores = jnp.einsum(
        "qhc,khc->hqk", heads_view[0], heads_view[1], preferred_element_type=jnp.float32
    ) * head_size ** (-0.5)
    relative_bias_value = jnp.einsum(
        "zrp,ze->erp", bucket_onehot_mask, position_bias_rows, preferred_element_type=jnp.float32
    )
    return jnp.where(allowed[None], scores + relative_bias_value, masked_score)


def attend_forward(
    values, gain_row, qkv_weight, attn_weight, position_bias_rows, allowed, bucket_onehot_mask
):
    row_count = values.shape[0]
    inv_rms = rms_scale(values)
    normed = (values * inv_rms * gain_row).astype(jnp.bfloat16)
    qkv_rows = jnp.einsum(
        "td,jdf->jtf", normed, qkv_weight, preferred_element_type=jnp.float32
    ).astype(jnp.bfloat16)
    head_count = position_bias_rows.shape[1]
    head_size = qkv_rows.shape[2] // head_count
    heads_view = qkv_rows.reshape(3, row_count, head_count, head_size)
    scores = attend_scores(heads_view, position_bias_rows, allowed, bucket_onehot_mask)
    top_score = jnp.max(scores, axis=-1, keepdims=True)
    log_total = jnp.log(jnp.sum(jnp.exp(scores - top_score), axis=-1, keepdims=True)) + top_score
    attn_probs = jnp.exp(scores - log_total)
    context = jnp.einsum(
        "hqk,khc->qhc",
        attn_probs.astype(jnp.bfloat16),
        heads_view[2],
        preferred_element_type=jnp.float32,
    )
    context = context.astype(jnp.bfloat16).reshape(row_count, head_count * head_size)
    partial_value = jnp.dot(context, attn_weight, preferred_element_type=jnp.float32)
    return (inv_rms, normed, qkv_rows, log_total, context, partial_value)


def expert_forward(normed_ffn, route_pairs, router_weight, inner_weight, outer_weight):
    row_count, features = normed_ffn.shape
    experts = router_weight.shape[1]
    capacity = 3 * row_count // experts
    owners = lax.axis_size("dp")
    local_count = inner_weight.shape[0]
    logits = jnp.dot(normed_ffn, router_weight, preferred_element_type=jnp.float32)
    gate_values = jax.nn.softmax(jnp.take_along_axis(logits, route_pairs, axis=1), axis=-1)
    slot_index = route_slots(route_pairs, experts, capacity)
    copies = jnp.repeat(normed_ffn, 2, axis=0)
    buffer = jnp.zeros((experts * capacity, features), jnp.bfloat16).at[slot_index].set(copies)
    received = dispatch(buffer.reshape(owners, local_count * capacity, features))
    expert_rows = received.reshape(owners, local_count, capacity, features)
    pre_act = jnp.einsum(
        "secd,edf->secf", expert_rows, inner_weight, preferred_element_type=jnp.float32
    )
    activation = jax.nn.gelu(pre_act, approximate=True).astype(jnp.bfloat16)
    partial_value = jnp.einsum(
        "secf,efd->secd", activation, outer_weight, preferred_element_type=jnp.float32
    )
    returned = settle(partial_value.reshape(owners, local_count * capacity, features))
    returned = returned.reshape(experts * capacity, features)[slot_index].reshape(
        row_count, 2, features
    )
    moe_out = jnp.sum(returned.astype(jnp.float32) * gate_values[:, :, None], axis=1)
    saved_residuals = {
        "gates": gate_values,
        "slots": slot_index,
        "received": received,
        "pre_act": pre_act,
        "returned": returned,
        "pairs": route_pairs,
    }
    return (moe_out, saved_residuals)


def expert_backward(grad_out, saved_residuals, router_weight, inner_weight, outer_weight):
    row_count, features = grad_out.shape
    experts = router_weight.shape[1]
    capacity = 3 * row_count // experts
    owners = lax.axis_size("dp")
    local_count = inner_weight.shape[0]
    gate_values = saved_residuals["gates"]
    returned = saved_residuals["returned"].astype(jnp.float32)
    grad_gates = jnp.sum(returned * grad_out[:, None, :], axis=-1)
    grad_copies = (
        (gate_values[:, :, None] * grad_out[:, None, :])
        .astype(jnp.bfloat16)
        .reshape(2 * row_count, features)
    )
    buffer = (
        jnp.zeros((experts * capacity, features), jnp.bfloat16)
        .at[saved_residuals["slots"]]
        .set(grad_copies)
    )
    received_grad = dispatch(buffer.reshape(owners, local_count * capacity, features))
    received_grad = received_grad.reshape(owners, local_count, capacity, features)
    activation, gelu_back = jax.vjp(
        lambda pre_value: jax.nn.gelu(pre_value, approximate=True), saved_residuals["pre_act"]
    )
    grad_act = jnp.einsum(
        "secd,efd->secf", received_grad, outer_weight, preferred_element_type=jnp.float32
    )
    grad_pre = gelu_back(grad_act)[0].astype(jnp.bfloat16)
    expert_rows = saved_residuals["received"].reshape(owners, local_count, capacity, features)
    outer_grad = jnp.einsum(
        "secf,secd->efd",
        activation.astype(jnp.bfloat16),
        received_grad,
        preferred_element_type=jnp.float32,
    )
    inner_grad = jnp.einsum(
        "secd,secf->edf", expert_rows, grad_pre, preferred_element_type=jnp.float32
    )
    partial_value = jnp.einsum(
        "secf,edf->secd", grad_pre, inner_weight, preferred_element_type=jnp.float32
    )
    returned_grad = settle(partial_value.reshape(owners, local_count * capacity, features))
    returned_grad = returned_grad.reshape(experts * capacity, features)[
        saved_residuals["slots"]
    ].reshape(row_count, 2, features)
    selected_gradient = gate_values * (
        grad_gates - jnp.sum(gate_values * grad_gates, axis=-1, keepdims=True)
    )
    expert_ids = jnp.arange(experts, dtype=jnp.int32)
    grad_logits = jnp.sum(
        (saved_residuals["pairs"][:, :, None] == expert_ids).astype(jnp.float32)
        * selected_gradient[:, :, None],
        axis=1,
    ).astype(jnp.bfloat16)
    router_grad = jnp.einsum(
        "td,te->de", saved_residuals["normed_ffn"], grad_logits, preferred_element_type=jnp.float32
    )
    grad_normed = jnp.sum(returned_grad.astype(jnp.float32), axis=1) + jnp.einsum(
        "te,de->td", grad_logits, router_weight, preferred_element_type=jnp.float32
    )
    return (grad_normed, router_grad, inner_grad, outer_grad)


def attend_backward(
    grad_hidden,
    saved_residuals,
    qkv_weight,
    attn_weight,
    position_bias_rows,
    allowed,
    bucket_onehot_mask,
):
    qkv_rows = saved_residuals["qkv"]
    row_count = grad_hidden.shape[0]
    head_count = position_bias_rows.shape[1]
    head_size = qkv_rows.shape[2] // head_count
    heads_view = qkv_rows.reshape(3, row_count, head_count, head_size)
    grad_attn = grad_hidden.astype(jnp.bfloat16)
    attn_grad = jnp.einsum(
        "tf,td->fd", saved_residuals["context"], grad_attn, preferred_element_type=jnp.float32
    )
    grad_context = jnp.einsum(
        "td,fd->tf", grad_attn, attn_weight, preferred_element_type=jnp.float32
    )
    grad_context = grad_context.astype(jnp.bfloat16).reshape(row_count, head_count, head_size)
    attn_probs = jnp.exp(
        attend_scores(heads_view, position_bias_rows, allowed, bucket_onehot_mask)
        - saved_residuals["log_total"]
    )
    grad_probs = jnp.einsum(
        "qhc,khc->hqk", grad_context, heads_view[2], preferred_element_type=jnp.float32
    )
    score_gradient = (
        attn_probs * (grad_probs - jnp.sum(attn_probs * grad_probs, axis=-1, keepdims=True))
    ).astype(jnp.bfloat16)
    bias_grad = jnp.einsum(
        "ygf,rgf->ry", score_gradient, bucket_onehot_mask, preferred_element_type=jnp.float32
    )
    factor = head_size ** (-0.5)
    grad_query = (
        jnp.einsum(
            "hqk,khc->qhc", score_gradient, heads_view[1], preferred_element_type=jnp.float32
        )
        * factor
    )
    grad_key = (
        jnp.einsum(
            "hqk,qhc->khc", score_gradient, heads_view[0], preferred_element_type=jnp.float32
        )
        * factor
    )
    grad_value = jnp.einsum(
        "hqk,qhc->khc",
        attn_probs.astype(jnp.bfloat16),
        grad_context,
        preferred_element_type=jnp.float32,
    )
    grad_qkv = (
        jnp.stack([grad_query, grad_key, grad_value])
        .reshape(3, row_count, head_count * head_size)
        .astype(jnp.bfloat16)
    )
    qkv_grad = jnp.einsum(
        "td,jtf->jdf", saved_residuals["normed"], grad_qkv, preferred_element_type=jnp.float32
    )
    grad_normed = heads_total(
        jnp.einsum("jtf,jdf->td", grad_qkv, qkv_weight, preferred_element_type=jnp.float32)
    )
    return (grad_normed, attn_grad, bias_grad, qkv_grad)


def layer_forward(
    layer_in,
    gain_pair,
    qkv_weight,
    attn_weight,
    position_bias_rows,
    router_weight,
    inner_weight,
    outer_weight,
    route_pairs,
    segment_row,
):
    values = layer_in.astype(jnp.float32)
    allowed, bucket_onehot_mask = score_layout(segment_row)
    inv_rms, normed, qkv_rows, log_total, context, partial_value = attend_forward(
        values,
        gain_pair[0],
        qkv_weight,
        attn_weight,
        position_bias_rows,
        allowed,
        bucket_onehot_mask,
    )
    hidden = values + heads_total(partial_value)
    ffn_rms = rms_scale(hidden)
    normed_ffn = (hidden * ffn_rms * gain_pair[1]).astype(jnp.bfloat16)
    moe_out, saved_residuals = expert_forward(
        normed_ffn, route_pairs, router_weight, inner_weight, outer_weight
    )
    saved_residuals = dict(
        saved_residuals,
        values=values,
        inv_rms=inv_rms,
        normed=normed,
        qkv=qkv_rows,
        log_total=log_total,
        context=context,
        hidden=hidden,
        ffn_rms=ffn_rms,
        normed_ffn=normed_ffn,
        segment=segment_row,
    )
    return ((hidden + moe_out).astype(jnp.bfloat16), saved_residuals)


def layer_backward(
    grad_out,
    saved_residuals,
    gain_pair,
    qkv_weight,
    attn_weight,
    position_bias_rows,
    router_weight,
    inner_weight,
    outer_weight,
):
    grad_normed_ffn, router_grad, inner_grad, outer_grad = expert_backward(
        grad_out, saved_residuals, router_weight, inner_weight, outer_weight
    )
    grad_hidden, gain_ffn = norm_gradient_return(
        saved_residuals["hidden"], saved_residuals["ffn_rms"], gain_pair[1], grad_normed_ffn
    )
    grad_hidden = grad_out + grad_hidden
    allowed, bucket_onehot_mask = score_layout(saved_residuals["segment"])
    grad_normed, attn_grad, bias_grad, qkv_grad = attend_backward(
        grad_hidden,
        saved_residuals,
        qkv_weight,
        attn_weight,
        position_bias_rows,
        allowed,
        bucket_onehot_mask,
    )
    grad_values, gain_attn = norm_gradient_return(
        saved_residuals["values"], saved_residuals["inv_rms"], gain_pair[0], grad_normed
    )
    pieces = {
        "gains": jnp.stack([gain_attn, gain_ffn]),
        "qkv": qkv_grad,
        "attn": attn_grad,
        "bias": bias_grad,
        "router": router_grad,
        "inner": inner_grad,
        "outer": outer_grad,
    }
    return (grad_hidden + grad_values, pieces)


def body(
    tokens,
    cotangent,
    norm_gains,
    w_qkv,
    w_attn_out,
    bias_table,
    router,
    w_in,
    w_out,
    routes,
    segments,
):
    section_index = lax.axis_index("section")
    is_first = section_index == 0
    micro_count, row_count = segments.shape
    features = tokens.shape[1]
    gain_pair = norm_gains[0].astype(jnp.float32)
    incoming = jnp.zeros((row_count, features), jnp.bfloat16)
    results = []
    stored_all = []
    for moment in range(micro_count + 1):
        batch_index = jnp.clip(moment - section_index, 0, micro_count - 1)
        own_rows = lax.dynamic_slice_in_dim(tokens, batch_index * row_count, row_count, 0)
        layer_in = jnp.where(is_first, own_rows, incoming)
        route_pairs = lax.dynamic_slice_in_dim(routes[0], batch_index * row_count, row_count, 0)
        segment_row = lax.dynamic_index_in_dim(segments, batch_index, 0, keepdims=False)
        layer_out, saved_residuals = layer_forward(
            layer_in,
            gain_pair,
            w_qkv[0],
            w_attn_out[0],
            bias_table[0],
            router[0],
            w_in[0],
            w_out[0],
            route_pairs,
            segment_row,
        )
        results.append(layer_out)
        stored_all.append(saved_residuals)
        if moment < micro_count:
            incoming = from_behind(layer_out, "section", 1)
    grad_carry = jnp.zeros((row_count, features), jnp.bfloat16)
    totals = None
    grads_in = []
    for moment in range(micro_count + 1):
        later_batch = min(moment, micro_count - 1)
        early_batch = max(moment - 1, 0)
        saved_residuals = jax.tree.map(
            lambda former, latter: jnp.where(is_first, former, latter),
            stored_all[early_batch],
            stored_all[later_batch + 1],
        )
        if moment < micro_count:
            supplied = cotangent[moment * row_count : (moment + 1) * row_count].astype(jnp.float32)
        else:
            supplied = jnp.zeros((row_count, features), jnp.float32)
        grad_out = jnp.where(is_first, grad_carry.astype(jnp.float32), supplied)
        grad_in, pieces = layer_backward(
            grad_out,
            saved_residuals,
            gain_pair,
            w_qkv[0],
            w_attn_out[0],
            bias_table[0],
            router[0],
            w_in[0],
            w_out[0],
        )
        totals = pieces if totals is None else jax.tree.map(jnp.add, totals, pieces)
        grads_in.append(grad_in)
        if moment < micro_count:
            grad_carry = from_behind(grad_in.astype(jnp.bfloat16), "section", -1)
    dense = (
        lax.psum(totals["gains"].astype(jnp.bfloat16), "dp").astype(jnp.float32),
        lax.psum(totals["qkv"].astype(jnp.bfloat16), "dp").astype(jnp.float32),
        lax.psum(totals["attn"].astype(jnp.bfloat16), "dp").astype(jnp.float32),
        lax.psum(totals["bias"].astype(jnp.bfloat16), "dp").astype(jnp.float32),
        lax.psum(totals["router"].astype(jnp.bfloat16), "dp").astype(jnp.float32),
    )
    out_rows = []
    grad_rows = []
    for micro_index in range(micro_count):
        out_rows.append(jnp.where(is_first, results[micro_index], results[micro_index + 1]))
        grad_rows.append(jnp.where(is_first, grads_in[micro_index + 1], grads_in[micro_index]))
    activations = jnp.concatenate(out_rows, axis=0)
    input_grads = jnp.concatenate(grad_rows, axis=0)
    return (
        activations[None],
        input_grads[None],
        dense[0][None],
        dense[1][None],
        dense[2][None],
        dense[3][None],
        dense[4][None],
        totals["inner"][None],
        totals["outer"][None],
    )


def solution(mesh):
    in_specs = (
        P("dp", None),
        P("dp", None),
        P("section", None, None),
        P("section", None, None, "tensor"),
        P("section", "tensor", None),
        P("section", None, "tensor"),
        P("section", None, None),
        P("section", "dp", None, "tensor"),
        P("section", "dp", "tensor", None),
        P("section", "dp", None),
        P("dp", None),
    )
    out_specs = (
        P("section", "dp", None),
        P("section", "dp", None),
        P("section", None, None),
        P("section", None, None, "tensor"),
        P("section", "tensor", None),
        P("section", None, "tensor"),
        P("section", None, None),
        P("section", "dp", None, "tensor"),
        P("section", "dp", "tensor", None),
    )
    return jax.shard_map(body, mesh=mesh, in_specs=in_specs, out_specs=out_specs, check_vma=False)
```

profile of v0, /device:TPU:0, one launch (start us, length us, event | category | flops | bytes accessed | tf_op | source)
XLA Modules:
  0.0 842.9 jit_solution(2025941584891993909)
XLA Ops:
  31.2 31.4 %all-reduce.16.cloned.1.call-done = bf16[128,768]{1,0:T(8,128)(2,1)} async-done(((bf16[128,768]{1,0:T(8,128)(2,1)}), bf16[128,768]{1,0:T(8,128)(2,1)}) %all-reduce.16.cloned.1.call-update) | async-done | bytes 196624 | tf_op jit(solution)/shard_map/psum | solution.py:45
  67.7 2.9 scatter_custom_fusion
  70.6 6.9 all-to-all-start
  81.1 6.8 all-to-all-done
  94.1 31.5 %all-reduce.27 = bf16[16,24,768]{2,1,0:T(8,128)(2,1)} all-reduce(f32[16,24,768]{2,1,0:T(8,128)} %copy.318), channel_id=1, replica_groups=mesh['section'=2,'dp'=16,'tensor'=4] {'tensor'}, use_global_device_ids=true, to_apply=%region_8.9 | all-reduce | flops 294912 | bytes 1769472 | tf_op jit(solution)/shard_map/psum | solution.py:53
  125.7 3.7 all-to-all-start.1
  130.3 9.5 %all-to-all-done.1 = bf16[16,24,768]{2,1,0:T(8,128)(2,1)S(1)} async-done(((bf16[16,24,768]{2,1,0:T(8,128)(2,1)}), bf16[16,24,768]{2,1,0:T(8,128)(2,1)S(1)}, u32[]{:S(2)}, u32[]{:S(2)}) %all-to-all-start.1) | async-done | bytes 589856 | tf_op jit(solution)/shard_map/all_to_all | solution.py:54
  153.1 38.1 %all-reduce.18.cloned.1.call-done = bf16[128,768]{1,0:T(8,128)(2,1)} async-done(((bf16[128,768]{1,0:T(8,128)(2,1)}), bf16[128,768]{1,0:T(8,128)(2,1)}) %all-reduce.18.cloned.1.call-update) | async-done | bytes 196624 | tf_op jit(solution)/shard_map/psum | solution.py:45
  201.5 6.8 all-to-all-start.2
  212.6 3.1 scatter_custom_fusion.3
  215.7 3.0 all-to-all-done.2
  218.8 4.5 all-to-all-start.6
  228.5 5.2 all-to-all-done.6
  235.2 2.7 fusion.52
  242.3 45.1 %all-reduce.28 = (bf16[16,24,768]{2,1,0:T(8,128)(2,1)}, bf16[16,24,768]{2,1,0:T(8,128)(2,1)}) all-reduce(f32[16,24,768]{2,1,0:T(8,128)} %copy.326, f32[16,24,768]{2,1,0:T(8,128)} %copy.340), channel_id=1, replica_groups=mesh['section'=2,'dp'=16,'tensor'=4] {'tensor'}, use_global_device_ids=true, to_apply=%region_20.22 | all-reduce | flops 589824 | bytes 3538944 | tf_op jit(solution)/shard_map/psum | solution.py:53
  287.4 3.7 all-to-all-start.3
  296.6 5.4 all-to-all-done.3
  302.0 4.2 all-to-all-start.7
  306.3 4.5 fusion.138
  316.7 2.7 gather_fusion.3
  331.1 2.8 reduce_sum.480
  351.3 38.9 %all-reduce.26.cloned.1.call-done = (bf16[128,768]{1,0:T(8,128)(2,1)}, bf16[128,768]{1,0:T(8,128)(2,1)}) async-done(((bf16[128,768]{1,0:T(8,128)(2,1)}, bf16[128,768]{1,0:T(8,128)(2,1)}), (bf16[128,768]{1,0:T(8,128)(2,1)}, bf16[128,768]{1,0:T(8,128)(2,1)})) %all-reduce.26.cloned.1.call-update) | async-done | bytes 393232 | tf_op jit(solution)/shard_map/psum | solution.py:45
  401.5 3.0 scatter_custom_fusion.2
  404.4 6.9 all-to-all-start.4
  417.1 3.2 scatter_custom_fusion.4
  420.3 3.9 all-to-all-done.4
  424.2 4.4 all-to-all-start.8
  436.4 3.0 fusion.365
  447.7 49.0 %all-reduce.29 = (bf16[16,24,768]{2,1,0:T(8,128)(2,1)}, bf16[16,24,768]{2,1,0:T(8,128)(2,1)}) all-reduce(f32[16,24,768]{2,1,0:T(8,128)} %copy.348, f32[16,24,768]{2,1,0:T(8,128)} %copy.334), channel_id=1, replica_groups=mesh['section'=2,'dp'=16,'tensor'=4] {'tensor'}, use_global_device_ids=true, to_apply=%region_48.50 | all-reduce | flops 589824 | bytes 3538944 | tf_op jit(solution)/shard_map/psum | solution.py:53
  496.8 4.9 all-to-all-start.5
  501.7 4.5 fusion.139
  506.2 7.3 all-to-all-done.5
  514.3 3.8 all-to-all-start.9
  518.4 4.3 fusion.366
  522.7 3.4 gather_fusion.2
  535.1 2.9 reduce_sum.488
  563.3 38.0 %all-reduce.20.cloned.1.call-done = bf16[128,768]{1,0:T(8,128)(2,1)} async-done(((bf16[128,768]{1,0:T(8,128)(2,1)}), bf16[128,768]{1,0:T(8,128)(2,1)}) %all-reduce.20.cloned.1.call-update) | async-done | bytes 196624 | tf_op jit(solution)/shard_map/psum | solution.py:45
  616.6 7.0 all-to-all-start.10
  628.1 8.1 all-to-all-done.10
  642.0 32.6 %all-reduce.30 = bf16[16,24,768]{2,1,0:T(8,128)(2,1)} all-reduce(f32[16,24,768]{2,1,0:T(8,128)} %copy.356), channel_id=1, replica_groups=mesh['section'=2,'dp'=16,'tensor'=4] {'tensor'}, use_global_device_ids=true, to_apply=%region_59.61 | all-reduce | flops 294912 | bytes 1769472 | tf_op jit(solution)/shard_map/psum | solution.py:53
  674.6 4.3 all-to-all-start.11
  678.9 7.5 fusion
  686.5 2.9 all-to-all-done.11
  693.7 2.8 reduce_sum.496
  702.2 3.5 fusion.44
  707.6 33.3 %all-reduce.22.cloned.1.call-done = bf16[128,768]{1,0:T(8,128)(2,1)} async-done(((bf16[128,768]{1,0:T(8,128)(2,1)}), bf16[128,768]{1,0:T(8,128)(2,1)}) %all-reduce.22.cloned.1.call-update) | async-done | bytes 196624 | tf_op jit(solution)/shard_map/psum | solution.py:45
  742.7 7.2 fusion.1
  749.9 75.9 %all-reduce.2 = (bf16[1,16,3]{1,2,0:T(4,128)(2,1)}, bf16[1,2,768]{2,1,0:T(2,128)(2,1)S(1)}, bf16[1,768,32]{1,2,0:T(8,128)(2,1)}) all-reduce(bf16[1,16,3]{1,2,0:T(4,128)(2,1)} %fusion.133, bf16[1,2,768]{2,1,0:T(2,128)(2,1)S(1)} %fusion.293, bf16[1,768,32]{1,2,0:T(8,128)(2,1)} %fusion.126), channel_id=1, replica_groups=mesh['section'=2,'dp'=16,'tensor'=4] {'dp'}, use_global_device_ids=true, to_apply=%region_78.80 | all-reduce | flops 26160 | bytes 104640 | tf_op jit(solution)/shard_map/psum | solution.py:443
  (655 shorter events, 235.0 us)
Async XLA Ops:
  7.2 84.2 %copy-start = (bf16[1,2,768,768]{3,2,1,0:T(8,128)(2,1)S(1)}, bf16[1,2,768,768]{3,2,1,0:T(8,128)(2,1)}, u32[]{:S(2)}) copy-start(bf16[1,2,768,768]{3,2,1,0:T(8,128)(2,1)} %param.27) | copy-start | bytes 7077892
  7.2 55.5 %all-reduce.16.cloned.1.call-start = ((), (), s32[]{:S(2)}) async-start(), calls=%async_computation.12 | async-start | bytes 393216 | tf_op jit(solution)/shard_map/psum | solution.py:45
  24.3 53.1 %copy-start.168 = (s32[256,1]{0,1:T(1,128)}, s32[256,1]{0,1:T(1,128)S(1)}, u32[]{:S(2)}) copy-start(s32[256,1]{0,1:T(1,128)S(1)} %get-tuple-element.160) | copy-start | bytes 3076
  27.5 35.1 %copy-start.10 = (bf16[256,768]{1,0:T(8,128)(2,1)S(1)}, bf16[256,768]{1,0:T(8,128)(2,1)}, u32[]{:S(2)}) copy-start(bf16[256,768]{1,0:T(8,128)(2,1)} %param.19) | copy-start | bytes 1179652
  63.7 128.5 %copy-start.152 = (f32[128]{0:T(128)}, f32[128]{0:T(128)S(1)}, u32[]{:S(2)}) copy-start(f32[128]{0:T(128)S(1)} %multiply_reduce_fusion.14) | copy-start | bytes 1540
  64.8 13.9 %copy-start.42 = (bf16[128,768]{1,0:T(8,128)(2,1)}, bf16[128,768]{1,0:T(8,128)(2,1)S(1)}, u32[]{:S(2)}) copy-start(bf16[128,768]{1,0:T(8,128)(2,1)S(1)} %multiply_convert_fusion.14) | copy-start | bytes 589828
  65.8 13.0 %copy-start.52 = (bf16[1,768,32]{1,2,0:T(8,128)(2,1)S(1)}, bf16[1,768,32]{1,2,0:T(8,128)(2,1)}, u32[]{:S(2)}) copy-start(bf16[1,768,32]{1,2,0:T(8,128)(2,1)} %param.25) | copy-start | bytes 147460
  70.6 17.4 %all-to-all-start = ((bf16[16,24,768]{2,1,0:T(8,128)(2,1)}), bf16[16,24,768]{2,1,0:T(8,128)(2,1)}, u32[]{:S(2)}, u32[]{:S(2)}) async-start(bf16[16,24,768]{2,1,0:T(8,128)(2,1)} %bitcast.471), calls=%async_computation | async-start | bytes 1179648 | tf_op jit(solution)/shard_map/all_to_all | solution.py:49
  125.7 14.1 %all-to-all-start.1 = ((bf16[16,24,768]{2,1,0:T(8,128)(2,1)}), bf16[16,24,768]{2,1,0:T(8,128)(2,1)S(1)}, u32[]{:S(2)}, u32[]{:S(2)}) async-start(bf16[16,24,768]{2,1,0:T(8,128)(2,1)} %all-reduce.27), calls=%async_computation.1 | async-start | bytes 1179648 | tf_op jit(solution)/shard_map/all_to_all | solution.py:54
  129.3 61.9 %all-reduce.18.cloned.1.call-start = ((), (), s32[]{:S(2)}) async-start(), calls=%async_computation.13 | async-start | bytes 393216 | tf_op jit(solution)/shard_map/psum | solution.py:45
  129.6 12.3 %copy-start.124 = (f32[128,2]{0,1:T(2,128)}, f32[128,2]{0,1:T(2,128)S(1)}, u32[]{:S(2)}) copy-start(f32[128,2]{0,1:T(2,128)S(1)} %get-tuple-element.129) | copy-start | bytes 3076
  129.6 12.3 %copy-start.130 = (f32[128]{0:T(128)}, f32[128]{0:T(128)S(1)}, u32[]{:S(2)}) copy-start(f32[128]{0:T(128)S(1)} %get-tuple-element.128) | copy-start | bytes 1540
  146.5 2.5 collective-permute-start
  151.4 44.6 %copy-start.128 = (f32[3,128]{1,0:T(4,128)}, f32[3,128]{1,0:T(4,128)S(1)}, u32[]{:S(2)}) copy-start(f32[3,128]{1,0:T(4,128)S(1)} %get-tuple-element.116) | copy-start | bytes 4612
  151.6 44.5 %copy-start.75 = (bf16[3,64,128]{2,1,0:T(8,128)(2,1)}, bf16[3,64,128]{2,1,0:T(8,128)(2,1)S(1)}, u32[]{:S(2)}) copy-start(bf16[3,64,128]{2,1,0:T(8,128)(2,1)S(1)} %convolution_convert_fusion.7) | copy-start | bytes 147460
  201.5 17.3 %all-to-all-start.2 = ((bf16[16,24,768]{2,1,0:T(8,128)(2,1)}), bf16[16,24,768]{2,1,0:T(8,128)(2,1)S(1)}, u32[]{:S(2)}, u32[]{:S(2)}) async-start(bf16[16,24,768]{2,1,0:T(8,128)(2,1)} %bitcast.470), calls=%async_computation.2 | async-start | bytes 1179648 | tf_op jit(solution)/shard_map/all_to_all | solution.py:49
  218.8 14.9 %all-to-all-start.6 = ((bf16[16,24,768]{2,1,0:T(8,128)(2,1)}), bf16[16,24,768]{2,1,0:T(8,128)(2,1)}, u32[]{:S(2)}, u32[]{:S(2)}) async-start(bf16[16,24,768]{2,1,0:T(8,128)(2,1)} %bitcast.472), calls=%async_computation.6 | async-start | bytes 1179648 | tf_op jit(solution)/shard_map/all_to_all | solution.py:49
  287.4 14.6 %all-to-all-start.3 = ((bf16[16,24,768]{2,1,0:T(8,128)(2,1)}), bf16[16,24,768]{2,1,0:T(8,128)(2,1)S(1)}, u32[]{:S(2)}, u32[]{:S(2)}) async-start(bf16[16,24,768]{2,1,0:T(8,128)(2,1)} %get-tuple-element.80), calls=%async_computation.3 | async-start | bytes 1179648 | tf_op jit(solution)/shard_map/all_to_all | solution.py:54
  302.0 14.7 %all-to-all-start.7 = ((bf16[16,24,768]{2,1,0:T(8,128)(2,1)}), bf16[16,24,768]{2,1,0:T(8,128)(2,1)}, u32[]{:S(2)}, u32[]{:S(2)}) async-start(bf16[16,24,768]{2,1,0:T(8,128)(2,1)} %get-tuple-element.81), calls=%async_computation.7 | async-start | bytes 1179648 | tf_op jit(solution)/shard_map/all_to_all | solution.py:54
  306.3 84.0 %all-reduce.26.cloned.1.call-start = ((), (), s32[]{:S(2)}) async-start(), calls=%async_computation.17 | async-start | bytes 786432 | tf_op jit(solution)/shard_map/psum | solution.py:45
  328.6 9.0 %collective-permute-start.1 = (bf16[128,768]{1,0:T(8,128)(2,1)}, bf16[128,768]{1,0:T(8,128)(2,1)}, u32[]{:S(2)}, u32[]{:S(2)}) collective-permute-start(bf16[128,768]{1,0:T(8,128)(2,1)} %get-tuple-element.110), channel_id=1, source_target_pairs={{0,64},{1,65},{2,66},{3,67},{4,68},{5,69},{6,70},{7,71},{8,72},{9,... | collective-permute-start | bytes 589832 | tf_op jit(solution)/shard_map/ppermute | solution.py:14
  348.7 42.6 %copy-start.153 = (f32[128]{0:T(128)S(1)}, f32[128]{0:T(128)}, u32[]{:S(2)}) copy-start(f32[128]{0:T(128)} %copy-done.152) | copy-start | bytes 1540
  348.7 42.6 %copy-start.155 = (f32[128]{0:T(128)S(1)}, f32[128]{0:T(128)}, u32[]{:S(2)}) copy-start(f32[128]{0:T(128)} %copy-done.154) | copy-start | bytes 1540
  348.7 43.1 %copy-start.149 = (f32[128]{0:T(128)S(1)}, f32[128]{0:T(128)}, u32[]{:S(2)}) copy-start(f32[128]{0:T(128)} %get-tuple-element.164) | copy-start | bytes 1540
  351.3 42.9 %copy-start.53 = (bf16[1,768,32]{1,2,0:T(8,128)(2,1)S(1)}, bf16[1,768,32]{1,2,0:T(8,128)(2,1)}, u32[]{:S(2)}) copy-start(bf16[1,768,32]{1,2,0:T(8,128)(2,1)} %param.25) | copy-start | bytes 147460
  397.1 14.2 %copy-start.140 = (f32[128,2]{0,1:T(2,128)}, f32[128,2]{0,1:T(2,128)S(1)}, u32[]{:S(2)}) copy-start(f32[128,2]{0,1:T(2,128)S(1)} %get-tuple-element.114) | copy-start | bytes 3076
  399.0 14.6 %collective-permute-start.2 = (bf16[128,768]{1,0:T(8,128)(2,1)}, bf16[128,768]{1,0:T(8,128)(2,1)}, u32[]{:S(2)}, u32[]{:S(2)}) collective-permute-start(bf16[128,768]{1,0:T(8,128)(2,1)} %fusion.346), channel_id=1, source_target_pairs={{64,0},{65,1},{66,2},{67,3},{68,4},{69,5},{70,6},{71,7},{72,8},{73... | collective-permute-start | bytes 589832 | tf_op jit(solution)/shard_map/ppermute | solution.py:14
  400.6 10.8 %copy-start.125 = (f32[128,2]{0,1:T(2,128)S(1)}, f32[128,2]{0,1:T(2,128)}, u32[]{:S(2)}) copy-start(f32[128,2]{0,1:T(2,128)} %copy-done.124) | copy-start | bytes 3076
  400.6 10.8 %copy-start.131 = (f32[128]{0:T(128)S(1)}, f32[128]{0:T(128)}, u32[]{:S(2)}) copy-start(f32[128]{0:T(128)} %copy-done.130) | copy-start | bytes 1540
  401.5 12.2 %copy-start.70 = (bf16[256,768]{1,0:T(8,128)(2,1)S(1)}, bf16[256,768]{1,0:T(8,128)(2,1)}, u32[]{:S(2)}) copy-start(bf16[256,768]{1,0:T(8,128)(2,1)} %param.20) | copy-start | bytes 1179652
  404.4 19.7 %all-to-all-start.4 = ((bf16[16,24,768]{2,1,0:T(8,128)(2,1)}), bf16[16,24,768]{2,1,0:T(8,128)(2,1)}, u32[]{:S(2)}, u32[]{:S(2)}) async-start(bf16[16,24,768]{2,1,0:T(8,128)(2,1)} %bitcast.66), calls=%async_computation.4 | async-start | bytes 1179648 | tf_op jit(solution)/shard_map/all_to_all | solution.py:49
  417.1 11.5 %copy-start.30 = (bf16[16,24,768]{2,1,0:T(8,128)(2,1)S(1)}, bf16[16,24,768]{2,1,0:T(8,128)(2,1)}, u32[]{:S(2)}) copy-start(bf16[16,24,768]{2,1,0:T(8,128)(2,1)} %copy-done.29) | copy-start | bytes 1769476
  424.2 17.8 %all-to-all-start.8 = ((bf16[16,24,768]{2,1,0:T(8,128)(2,1)}), bf16[16,24,768]{2,1,0:T(8,128)(2,1)}, u32[]{:S(2)}, u32[]{:S(2)}) async-start(bf16[16,24,768]{2,1,0:T(8,128)(2,1)} %bitcast.468), calls=%async_computation.8 | async-start | bytes 1179648 | tf_op jit(solution)/shard_map/all_to_all | solution.py:49
  496.8 16.7 %all-to-all-start.5 = ((bf16[16,24,768]{2,1,0:T(8,128)(2,1)}), bf16[16,24,768]{2,1,0:T(8,128)(2,1)S(1)}, u32[]{:S(2)}, u32[]{:S(2)}) async-start(bf16[16,24,768]{2,1,0:T(8,128)(2,1)} %get-tuple-element.79), calls=%async_computation.5 | async-start | bytes 1179648 | tf_op jit(solution)/shard_map/all_to_all | solution.py:54
  514.3 16.5 %all-to-all-start.9 = ((bf16[16,24,768]{2,1,0:T(8,128)(2,1)}), bf16[16,24,768]{2,1,0:T(8,128)(2,1)S(1)}, u32[]{:S(2)}, u32[]{:S(2)}) async-start(bf16[16,24,768]{2,1,0:T(8,128)(2,1)} %get-tuple-element.78), calls=%async_computation.9 | async-start | bytes 1179648 | tf_op jit(solution)/shard_map/all_to_all | solution.py:54
  518.1 83.2 %all-reduce.20.cloned.1.call-start = ((), (), s32[]{:S(2)}) async-start(), calls=%async_computation.14 | async-start | bytes 393216 | tf_op jit(solution)/shard_map/psum | solution.py:45
  561.4 41.0 %copy-start.18 = (f32[128,768]{1,0:T(8,128)S(1)}, f32[128,768]{1,0:T(8,128)}, u32[]{:S(2)}) copy-start(f32[128,768]{1,0:T(8,128)} %copy-done.17) | copy-start | bytes 1179652
  604.8 3.5 collective-permute-start.3
  616.6 19.6 %all-to-all-start.10 = ((bf16[16,24,768]{2,1,0:T(8,128)(2,1)}), bf16[16,24,768]{2,1,0:T(8,128)(2,1)}, u32[]{:S(2)}, u32[]{:S(2)}) async-start(bf16[16,24,768]{2,1,0:T(8,128)(2,1)} %bitcast.469), calls=%async_computation.10 | async-start | bytes 1179648 | tf_op jit(solution)/shard_map/all_to_all | solution.py:49
  674.6 14.7 %all-to-all-start.11 = ((bf16[16,24,768]{2,1,0:T(8,128)(2,1)}), bf16[16,24,768]{2,1,0:T(8,128)(2,1)S(1)}, u32[]{:S(2)}, u32[]{:S(2)}) async-start(bf16[16,24,768]{2,1,0:T(8,128)(2,1)} %all-reduce.30), calls=%async_computation.11 | async-start | bytes 1179648 | tf_op jit(solution)/shard_map/all_to_all | solution.py:54
  678.9 62.1 %all-reduce.22.cloned.1.call-start = ((), (), s32[]{:S(2)}) async-start(), calls=%async_computation.15 | async-start | bytes 393216 | tf_op jit(solution)/shard_map/psum | solution.py:45
  701.8 130.5 %all-reduce.24.cloned.1.call-start = ((), (), s32[]{:S(2)}) async-start(), calls=%async_computation.16 | async-start | bytes 2359296 | tf_op jit(solution)/shard_map/psum | solution.py:441
  706.7 34.3 %copy-start.158 = (f32[128]{0:T(128)S(1)}, f32[128]{0:T(128)}, u32[]{:S(2)}) copy-start(f32[128]{0:T(128)} %get-tuple-element.162) | copy-start | bytes 1540
  707.6 35.0 %copy-start.132 = (f32[1,768]{1,0:T(1,128)S(1)}, f32[1,768]{1,0:T(1,128)}, u32[]{:S(2)}) copy-start(f32[1,768]{1,0:T(1,128)} %stack.76) | copy-start | bytes 9220
  707.6 35.0 %copy-start.133 = (f32[1,768]{1,0:T(1,128)S(1)}, f32[1,768]{1,0:T(1,128)}, u32[]{:S(2)}) copy-start(f32[1,768]{1,0:T(1,128)} %stack.79) | copy-start | bytes 9220
  707.6 35.0 %copy-start.134 = (f32[1,768]{1,0:T(1,128)S(1)}, f32[1,768]{1,0:T(1,128)}, u32[]{:S(2)}) copy-start(f32[1,768]{1,0:T(1,128)} %stack.78) | copy-start | bytes 9220
  742.7 87.1 %copy-start.49 = (f32[128,768]{1,0:T(8,128)S(1)}, f32[128,768]{1,0:T(8,128)}, u32[]{:S(2)}) copy-start(f32[128,768]{1,0:T(8,128)} %copy-done.48) | copy-start | bytes 1179652
  742.7 87.1 %copy-start.159 = (f32[128]{0:T(128)S(1)}, f32[128]{0:T(128)}, u32[]{:S(2)}) copy-start(f32[128]{0:T(128)} %get-tuple-element.162) | copy-start | bytes 1540
  (152 other events, 463.3 us)
Sparse Core Ops, SparseCore 0:
  18.4 44.1 all-reduce.15
  152.6 38.5 all-reduce.17
  348.2 41.9 all-reduce.25
  559.4 41.8 all-reduce.19
  701.9 38.9 all-reduce.21
  745.0 87.2 all-reduce.23
where the time goes:
time: 854 us; the launch traced here: 843 us
  waiting for transfers between devices  237 us (28%)
  blocking collectives  234 us (27%)
  local copies, waits for them, and re-layouts  111 us (13%)
  other arithmetic  90.5 us (11%)
  matrix products  85 us (10%)
  starting transfers between devices  68.8 us (8%)
  between operations  17.1 us (2%)
    psum x5, waiting for transfers between devices, heads_total(): lax.psum(partial_value.astype(jnp.bfloat16), 'tensor').astype(jnp.float32)  180 us
    psum x4, blocking collectives, settle(): summed = lax.psum(partial_value, 'tensor').astype(jnp.bfloat16)  158 us
    psum x1, blocking collectives, body(): lax.psum(totals['bias'].astype(jnp.bfloat16), 'dp').astype(jnp.float32)  75.9 us
    all_to_all x6, starting transfers between devices, dispatch(): return lax.all_to_all(buffer, 'dp', split_axis=0, concat_axis=0, tiled=True)  36.4 us
    all_to_all x6, waiting for transfers between devices, dispatch(): return lax.all_to_all(buffer, 'dp', split_axis=0, concat_axis=0, tiled=True)  29.7 us
    all_to_all x6, waiting for transfers between devices, settle(): return lax.all_to_all(summed, 'dp', split_axis=0, concat_axis=0, tiled=True)  25.6 us
    all_to_all x6, starting transfers between devices, settle(): return lax.all_to_all(summed, 'dp', split_axis=0, concat_axis=0, tiled=True)  24.6 us
  transfers between devices with their start and end apart: 22, of which 19 were waited for; matrix products, arithmetic and copies ran while one was open for 15% of the time, Pallas kernels for 0%

commit v1 on v0

v1 whole, which is shorter than its diff:
```python
import jax
import jax.numpy as jnp
from jax import lax
from jax.experimental import pallas as pl
from jax.experimental.pallas import tpu as pltpu
from jax.sharding import PartitionSpec as P

epsilon = 1e-06
masked_score = -1000000000.0
bucket_edges = (1, 2, 3, 4, 5, 6, 7, 8, 10, 13, 16, 20, 25, 32, 40)
MESH = pl.DeviceIdType.MESH
f32 = jnp.float32
bf16 = jnp.bfloat16

DP = 16
TZ = 4
ROWS = 256
BLOCK = 128
OWN = ROWS // TZ
D = 768
HF = 192
HEADS = 3
CAP = 12
MSG = 48
SLOTS = DP * MSG
ER = SLOTS // 2
SMALL = 128
GAIN0, GAIN1, BIAS = 33, 32, 34


def nn(a, b):
    return lax.dot_general(a, b, (((1,), (0,)), ((), ())), preferred_element_type=f32)


def nt(a, b):
    return lax.dot_general(a, b, (((1,), (1,)), ((), ())), preferred_element_type=f32)


def tn(a, b):
    return lax.dot_general(a, b, (((0,), (0,)), ((), ())), preferred_element_type=f32)


def iota(shape, dim):
    return lax.broadcasted_iota(jnp.int32, shape, dim)


def rms_scale(values):
    return lax.rsqrt(jnp.mean(values * values, axis=-1, keepdims=True) + epsilon)


def kernel(
    tokens, cotangent, gains, w_qkv, w_att, bias_tab, router, w_in_hbm, w_out_hbm, routes, segments,
    act_out, grad_out, dense_out, small_out, xe_out, u_out, dpre_out, de_out,
    xin, gin, w_in, w_out, wall, call, normed, qkv, probs, hidden, hid_scale, normed2, rpad,
    gate, slots, ptg, send_b, recv_b, send_e, recv_e, send_d, recv_d, send_x, recv_x,
    xe, act, dact, de, dpre, yf, part_y, rs_y, part_h, rs_h, dh_full, part_a, rs_a, in_full,
    dq_all, gact, dense_s, dense_r, dense_f, small_z, small_f,
    ld_sem, out_sem, w_ss, w_rs, c_ss, c_rs, b_ss, b_rs, e_ss, e_rs, d_ss, d_rs, x_ss, x_rs,
    ry_ss, ry_rs, ay_ss, ay_rs, rh_ss, rh_rs, ah_ss, ah_rs, ra_ss, ra_rs, aa_ss, aa_rs,
    hand_ss, hand_rs, back_ss, back_rs, dn_ss, dn_rs, df_ss, df_rs, sz_ss, sz_rs, sf_ss, sf_rs,
    turn_sem,
):
    sec = lax.axis_index("section")
    me = lax.axis_index("dp")
    mz = lax.axis_index("tensor")
    first = sec == 0

    load_in = pltpu.make_async_copy(w_in_hbm, w_in, ld_sem.at[0])
    load_out = pltpu.make_async_copy(w_out_hbm, w_out, ld_sem.at[1])
    load_in.start()
    load_out.start()

    barrier = pltpu.get_barrier_semaphore()

    def greet(i, carry):
        pl.semaphore_signal(
            barrier, inc=1, device_id={"dp": lax.rem(me + i, DP)}, device_id_type=MESH
        )
        return carry

    lax.fori_loop(1, DP, greet, 0)
    for i in range(1, TZ):
        pl.semaphore_signal(
            barrier, inc=1, device_id={"tensor": lax.rem(mz + i, TZ)}, device_id_type=MESH
        )
    pl.semaphore_signal(barrier, inc=1, device_id={"section": 1 - sec}, device_id_type=MESH)
    pl.semaphore_wait(barrier, DP + TZ - 1)

    def z_copy(src, dst, ss, rs, peer, slot):
        return pltpu.make_async_remote_copy(
            src_ref=src, dst_ref=dst, send_sem=ss.at[peer], recv_sem=rs.at[slot],
            device_id={"tensor": peer}, device_id_type=MESH,
        )

    def gather_start(buf, ss, rs):
        for i in range(1, TZ):
            z_copy(buf.at[mz], buf.at[mz], ss, rs, lax.rem(mz + i, TZ), mz).start()

    def gather_recv(buf, ss, rs, i):
        src = lax.rem(mz + i, TZ)
        z_copy(buf.at[src], buf.at[src], ss, rs, src, src).wait_recv()

    def gather_sent(buf, ss, rs):
        for i in range(1, TZ):
            z_copy(buf.at[mz], buf.at[mz], ss, rs, lax.rem(mz + i, TZ), mz).wait_send()

    def scatter_start(part, rcv, ss, rs):
        for i in range(1, TZ):
            peer = lax.rem(mz + i, TZ)
            z_copy(part.at[peer], rcv.at[mz], ss, rs, peer, mz).start()

    def scatter_sum(part, rcv, ss, rs):
        total = part[mz].astype(f32)
        for i in range(1, TZ):
            src = lax.rem(mz + i, TZ)
            z_copy(part.at[src], rcv.at[src], ss, rs, src, src).wait_recv()
            total += rcv[src].astype(f32)
        return total

    def scatter_sent(part, rcv, ss, rs):
        for i in range(1, TZ):
            peer = lax.rem(mz + i, TZ)
            z_copy(part.at[peer], rcv.at[mz], ss, rs, peer, mz).wait_send()

    def dp_copy(src, dst, ss, rs, peer, slot):
        return pltpu.make_async_remote_copy(
            src_ref=src, dst_ref=dst, send_sem=ss.at[peer], recv_sem=rs.at[slot],
            device_id={"dp": peer}, device_id_type=MESH,
        )

    def swap_one(snd, rcv, ss, rs, peer):
        @pl.when(peer != me)
        def _():
            dp_copy(snd.at[peer], rcv.at[me], ss, rs, peer, me).start()

    def swap_start(snd, rcv, ss, rs):
        rcv[me] = snd[me]

        def step(i, carry):
            swap_one(snd, rcv, ss, rs, lax.rem(me + i, DP))
            return carry

        lax.fori_loop(1, DP, step, 0)

    def swap_recv(snd, rcv, ss, rs, src):
        @pl.when(src != me)
        def _():
            dp_copy(snd.at[src], rcv.at[src], ss, rs, src, src).wait_recv()

    def swap_recv_all(snd, rcv, ss, rs):
        def step(i, carry):
            swap_recv(snd, rcv, ss, rs, lax.rem(me + DP - i, DP))
            return carry

        lax.fori_loop(1, DP, step, 0)

    def swap_sent(snd, rcv, ss, rs):
        def step(i, carry):
            peer = lax.rem(me + i, DP)
            dp_copy(snd.at[peer], rcv.at[me], ss, rs, peer, me).wait_send()
            return carry

        lax.fori_loop(1, DP, step, 0)

    def unpack(snd, rcv, ss, rs, rows):
        def step(i, carry):
            pair = lax.rem(me // 2 + DP // 2 - i, DP // 2)
            swap_recv(snd, rcv, ss, rs, 2 * pair)
            swap_recv(snd, rcv, ss, rs, 2 * pair + 1)
            one = rcv[2 * pair].astype(f32)
            two = rcv[2 * pair + 1].astype(f32)
            at = pl.ds(pl.multiple_of(pair * MSG, MSG), MSG)
            half = MSG // 2
            rows[0, at, :] = jnp.concatenate([one[:half], two[:half]], axis=0).astype(bf16)
            rows[1, at, :] = jnp.concatenate([one[half:], two[half:]], axis=0).astype(bf16)
            return carry

        lax.fori_loop(0, DP // 2, step, 0)

    def pack(snd, rcv, ss, rs):
        def step(i, carry):
            pair = lax.rem(me // 2 + i, DP // 2)
            at = pl.ds(pl.multiple_of(pair * MSG, MSG), MSG)
            half = MSG // 2
            one = yf[0, at, :]
            two = yf[1, at, :]
            snd[2 * pair] = jnp.concatenate([one[:half], two[:half]], axis=0).astype(bf16)
            snd[2 * pair + 1] = jnp.concatenate([one[half:], two[half:]], axis=0).astype(bf16)
            swap_one(snd, rcv, ss, rs, 2 * pair)
            swap_one(snd, rcv, ss, rs, 2 * pair + 1)
            return carry

        lax.fori_loop(0, DP // 2, step, 0)
        rcv[me] = snd[me]

    @pl.when(first)
    def _():
        wall[mz] = w_att[0]
        gather_start(wall, w_ss, w_rs)
        xin[...] = tokens[...].reshape(TZ, OWN, D)

    @pl.when(jnp.logical_not(first))
    def _():
        gin[...] = cotangent[...].reshape(TZ, OWN, D)
        pl.semaphore_wait(turn_sem, 1)
        wall[mz] = w_att[0]
        gather_start(wall, w_ss, w_rs)

    tok = iota((ROWS, ROWS), 0)
    oth = iota((ROWS, ROWS), 1)
    same = (tok // BLOCK) == (oth // BLOCK)
    earlier = (same & (tok > oth)).astype(f32).astype(bf16)
    within = same.astype(f32).astype(bf16)
    lane = iota((ROWS, SMALL), 1)
    e0 = routes[0][:, 0:1]
    e1 = routes[0][:, 1:2]
    hit0 = (lane == e0).astype(f32)
    hit1 = (lane == e1).astype(f32)
    rank0 = jnp.sum(nn(earlier, hit0.astype(bf16)) * hit0, axis=1, keepdims=True)
    rank1 = jnp.sum(
        (nn(earlier, hit1.astype(bf16)) + nn(within, hit0.astype(bf16))) * hit1,
        axis=1, keepdims=True,
    )
    base = (iota((ROWS, 1), 0) // BLOCK) * CAP
    slot0 = (e0 // 2) * MSG + (e0 % 2) * (MSG // 2) + base + rank0.astype(jnp.int32)
    slot1 = (e1 // 2) * MSG + (e1 % 2) * (MSG // 2) + base + rank1.astype(jnp.int32)
    slots[:, 0:1] = slot0
    slots[:, 1:2] = slot1
    rpad[...] = jnp.zeros((D, SMALL), bf16)
    rpad[:, 0:32] = router[0]

    @pl.when(jnp.logical_not(first))
    def _():
        for t in range(TZ):
            pltpu.make_async_remote_copy(
                src_ref=in_full.at[t], dst_ref=xin.at[t], send_sem=hand_ss.at[t],
                recv_sem=hand_rs.at[t], device_id={"section": 1 - sec}, device_id_type=MESH,
            ).wait_recv()

    x = xin[...].reshape(ROWS, D).astype(f32)
    gain0 = gains[0, 0:1, :].astype(f32)
    gain1 = gains[0, 1:2, :].astype(f32)
    normed[...] = (x * rms_scale(x) * gain0).astype(bf16)
    for j in range(3):
        qkv[j] = nn(normed[...], w_qkv[0, j]).astype(bf16)

    row = iota((BLOCK, BLOCK), 0)
    col = iota((BLOCK, BLOCK), 1)
    gap = row - col
    head_of = iota((BLOCK, HF), 1) // (HF // HEADS)
    bias_now = []
    for h in range(HEADS):
        value = jnp.broadcast_to(bias_tab[0, 0:1, h : h + 1].astype(f32), (BLOCK, BLOCK))
        for b, edge in enumerate(bucket_edges):
            value = jnp.where(gap >= edge, bias_tab[0, b + 1 : b + 2, h : h + 1].astype(f32), value)
        bias_now.append(value)
    for b in range(2):
        rows = slice(b * BLOCK, (b + 1) * BLOCK)
        seg_row = segments[b : b + 1, :].astype(f32)
        seg_col = jnp.sum(jnp.where(row == col, seg_row, 0.0), axis=1, keepdims=True)
        allowed = (gap >= 0) & (seg_row == seg_col)
        q = qkv[0, rows, :]
        k = qkv[1, rows, :]
        v = qkv[2, rows, :]
        context = jnp.zeros((BLOCK, HF), f32)
        for h in range(HEADS):
            score = nt(jnp.where(head_of == h, q, jnp.zeros_like(q)), k) * 0.125 + bias_now[h]
            score = jnp.where(allowed, score, masked_score)
            score = jnp.exp(score - jnp.max(score, axis=-1, keepdims=True))
            prob = score / jnp.sum(score, axis=-1, keepdims=True)
            probs[b * HEADS + h] = prob
            context = jnp.where(head_of == h, nn(prob.astype(bf16), v), context)
        call[mz, rows, :] = context.astype(bf16)
    gather_start(call, c_ss, c_rs)

    slot_lane = iota((ROWS, SLOTS), 1)
    eye = tok == oth
    row0 = jnp.sum(jnp.where(eye, slots[:, 0:1], 0), axis=0, keepdims=True)
    row1 = jnp.sum(jnp.where(eye, slots[:, 1:2], 0), axis=0, keepdims=True)
    slot_sub = iota((SLOTS, ROWS), 0)
    pick = ((slot_sub == row0) | (slot_sub == row1)).astype(f32).astype(bf16)

    for i in range(1, TZ):
        gather_recv(call, c_ss, c_rs, i)
        gather_recv(wall, w_ss, w_rs, i)

    @pl.when(first)
    def _():
        pl.semaphore_signal(turn_sem, inc=1, device_id={"section": 1 - sec}, device_id_type=MESH)

    h = xin[...].reshape(ROWS, D).astype(f32)
    for t in range(TZ):
        h += nn(call[t], wall[t])
    hidden[...] = h
    scale = rms_scale(h)
    hid_scale[...] = scale
    normed2[...] = (h * scale * gain1).astype(bf16)

    sent = nn(pick, normed2[...]).astype(bf16)
    send_b[...] = sent.reshape(DP, MSG, D)
    swap_start(send_b, recv_b, b_ss, b_rs)

    z = nn(normed2[...], rpad[...])
    z0 = jnp.sum(z * hit0, axis=1, keepdims=True)
    z1 = jnp.sum(z * hit1, axis=1, keepdims=True)
    g0 = 1.0 / (1.0 + jnp.exp(z1 - z0))
    g1 = 1.0 / (1.0 + jnp.exp(z0 - z1))
    gate[:, 0:1] = g0
    gate[:, 1:2] = g1
    ptg[...] = (
        jnp.where(slot_lane == slot0, g0, 0.0) + jnp.where(slot_lane == slot1, g1, 0.0)
    ).astype(bf16)

    def dispatch_grad():
        grow0 = jnp.sum(jnp.where(eye, gate[:, 0:1], 0.0), axis=0, keepdims=True)
        grow1 = jnp.sum(jnp.where(eye, gate[:, 1:2], 0.0), axis=0, keepdims=True)
        crow0 = jnp.sum(jnp.where(eye, slots[:, 0:1], 0), axis=0, keepdims=True)
        crow1 = jnp.sum(jnp.where(eye, slots[:, 1:2], 0), axis=0, keepdims=True)
        pick_g = jnp.where(slot_sub == crow0, grow0, 0.0) + jnp.where(slot_sub == crow1, grow1, 0.0)
        out = nn(pick_g.astype(bf16), gin[...].reshape(ROWS, D)).astype(bf16)
        send_d[...] = out.reshape(DP, MSG, D)
        swap_start(send_d, recv_d, d_ss, d_rs)

    @pl.when(jnp.logical_not(first))
    def _():
        dispatch_grad()

    unpack(send_b, recv_b, b_ss, b_rs, xe)
    load_in.wait()
    load_out.wait()
    save_xe = pltpu.make_async_copy(xe, xe_out, out_sem.at[0])
    save_xe.start()
    root = 0.7978845608028654

    def expert_forward(e, carry):
        for n in range(3):
            cols = slice(256 * n, 256 * (n + 1))
            pre = nn(xe[e], w_in[e, :, cols])
            square = pre * pre
            wave = jnp.tanh(root * pre * (1.0 + 0.044715 * square))
            lift = 0.5 * (1.0 + wave)
            act[e, :, cols] = (pre * lift).astype(bf16)
            slope = lift + 0.5 * root * pre * (1.0 - wave * wave) * (1.0 + 0.134145 * square)
            dact[e, :, cols] = slope.astype(bf16)
        yf[e] = nn(act[e], w_out[e])
        return carry

    lax.fori_loop(0, 2, expert_forward, 0)
    save_u = pltpu.make_async_copy(act, u_out, out_sem.at[1])
    save_u.start()
    pack(send_e, recv_e, e_ss, e_rs)

    def finish_forward():
        swap_recv_all(send_e, recv_e, e_ss, e_rs)
        part_y[...] = nn(ptg[...], recv_e[...].reshape(SLOTS, D)).astype(bf16).reshape(TZ, OWN, D)
        scatter_start(part_y, rs_y, ry_ss, ry_rs)
        own = pl.ds(pl.multiple_of(mz * OWN, OWN), OWN)
        total = scatter_sum(part_y, rs_y, ry_ss, ry_rs) + hidden[own, :]
        act_all = gact
        act_all[mz] = total.astype(bf16)
        gather_start(act_all, ay_ss, ay_rs)

    def hand(t, ss, rs, src, dst):
        return pltpu.make_async_remote_copy(
            src_ref=src.at[t], dst_ref=dst.at[t], send_sem=ss.at[t], recv_sem=rs.at[t],
            device_id={"section": 1 - sec}, device_id_type=MESH,
        )

    @pl.when(first)
    def _():
        finish_forward()
        hand(mz, hand_ss, hand_rs, gact, xin).start()
        for i in range(1, TZ):
            gather_recv(gact, ay_ss, ay_rs, i)
            hand(lax.rem(mz + i, TZ), hand_ss, hand_rs, gact, xin).start()
        for t in range(TZ):
            hand(t, back_ss, back_rs, in_full, gin).wait_recv()
        dispatch_grad()

    unpack(send_d, recv_d, d_ss, d_rs, de)
    save_de = pltpu.make_async_copy(de, de_out, out_sem.at[2])
    save_de.start()

    def expert_backward(e, carry):
        for n in range(3):
            cols = slice(256 * n, 256 * (n + 1))
            grad = nt(de[e], w_out[e, cols, :])
            dpre[e, :, cols] = (grad * dact[e, :, cols].astype(f32)).astype(bf16)
        yf[e] = nt(dpre[e], w_in[e])
        return carry

    lax.fori_loop(0, 2, expert_backward, 0)
    save_dpre = pltpu.make_async_copy(dpre, dpre_out, out_sem.at[3])
    save_dpre.start()
    pack(send_x, recv_x, x_ss, x_rs)

    @pl.when(jnp.logical_not(first))
    def _():
        finish_forward()
        for i in range(1, TZ):
            gather_recv(gact, ay_ss, ay_rs, i)

    act_out[...] = gact[...].reshape(ROWS, D)

    c0 = slots[:, 0:1]
    c1 = slots[:, 1:2]
    w0 = gate[:, 0:1]
    w1 = gate[:, 1:2]
    marks = nt(gin[...].reshape(ROWS, D), recv_e[...].reshape(SLOTS, D))
    dg0 = jnp.sum(jnp.where(slot_lane == c0, marks, 0.0), axis=1, keepdims=True)
    dg1 = jnp.sum(jnp.where(slot_lane == c1, marks, 0.0), axis=1, keepdims=True)
    mean = w0 * dg0 + w1 * dg1
    dz = (
        jnp.where(lane == routes[0][:, 0:1], w0 * (dg0 - mean), 0.0)
        + jnp.where(lane == routes[0][:, 1:2], w1 * (dg1 - mean), 0.0)
    ).astype(bf16)
    pick_t = ((slot_lane == c0) | (slot_lane == c1)).astype(f32).astype(bf16)

    swap_recv_all(send_x, recv_x, x_ss, x_rs)
    db = nn(pick_t, recv_x[...].reshape(SLOTS, D)) + nt(dz, rpad[...])
    part_h[...] = db.astype(bf16).reshape(TZ, OWN, D)
    scatter_start(part_h, rs_h, rh_ss, rh_rs)
    small = tn(normed2[...], dz)
    unit1 = (lane == GAIN1).astype(f32).astype(bf16)
    unit0 = (lane == GAIN0).astype(f32).astype(bf16)
    small += tn((db * hidden[...] * hid_scale[...]).astype(bf16), unit1)

    own = pl.ds(pl.multiple_of(mz * OWN, OWN), OWN)
    db_own = scatter_sum(part_h, rs_h, rh_ss, rh_rs)
    h_own = hidden[own, :]
    s_own = hid_scale[own, :]
    lifted = db_own * gain1
    hat = h_own * s_own
    dh_own = gin[mz].astype(f32) + s_own * (
        lifted - hat * jnp.mean(lifted * hat, axis=-1, keepdims=True)
    )
    dh_full[mz] = dh_own.astype(bf16)
    gather_start(dh_full, ah_ss, ah_rs)
    for i in range(1, TZ):
        gather_recv(dh_full, ah_ss, ah_rs, i)

    do = dh_full[...].reshape(ROWS, D)
    dc_all = nt(do, w_att[0]).astype(bf16)
    score_grads = [jnp.zeros((BLOCK, BLOCK), f32) for _ in range(HEADS)]
    for b in range(2):
        rows = slice(b * BLOCK, (b + 1) * BLOCK)
        q = qkv[0, rows, :]
        k = qkv[1, rows, :]
        v = qkv[2, rows, :]
        dc = dc_all[rows, :]
        dq = jnp.zeros((BLOCK, HF), f32)
        dk = jnp.zeros((BLOCK, HF), f32)
        dv = jnp.zeros((BLOCK, HF), f32)
        for h in range(HEADS):
            mine = head_of == h
            prob = probs[b * HEADS + h]
            dp = nt(jnp.where(mine, dc, jnp.zeros_like(dc)), v)
            ds = (prob * (dp - jnp.sum(prob * dp, axis=-1, keepdims=True))).astype(bf16)
            score_grads[h] += ds.astype(f32)
            dq = jnp.where(mine, nn(ds, k), dq)
            dk = jnp.where(mine, tn(ds, q), dk)
            dv = jnp.where(mine, tn(prob.astype(bf16), dc), dv)
        dq_all[0, rows, :] = (dq * 0.125).astype(bf16)
        dq_all[1, rows, :] = (dk * 0.125).astype(bf16)
        dq_all[2, rows, :] = dv.astype(bf16)
    da = nt(dq_all[0], w_qkv[0, 0]) + nt(dq_all[1], w_qkv[0, 1]) + nt(dq_all[2], w_qkv[0, 2])
    part_a[...] = da.astype(bf16).reshape(TZ, OWN, D)
    scatter_start(part_a, rs_a, ra_ss, ra_rs)

    xs = xin[...].reshape(ROWS, D).astype(f32)
    small += tn((da * xs * rms_scale(xs)).astype(bf16), unit0)
    bias_rows = []
    edges = (0,) + bucket_edges
    for b in range(len(edges)):
        hit = gap >= edges[b]
        if b + 1 < len(edges):
            hit = hit & (gap < edges[b + 1])
        for h in range(HEADS):
            bias_rows.append(jnp.sum(jnp.where(hit, score_grads[h], 0.0), axis=0, keepdims=True))
    bias_col = jnp.sum(jnp.concatenate(bias_rows, axis=0), axis=1, keepdims=True)
    lane48 = iota((MSG, SMALL), 1)
    bias_part = jnp.where(lane48 == BIAS + mz, bias_col, 0.0)

    a_own = scatter_sum(part_a, rs_a, ra_ss, ra_rs)
    x_own = xin[mz].astype(f32)
    r_own = rms_scale(x_own)
    lifted = a_own * gain0
    hat = x_own * r_own
    grad_own = dh_own + r_own * (lifted - hat * jnp.mean(lifted * hat, axis=-1, keepdims=True))
    in_full[mz] = grad_own.astype(bf16)
    gather_start(in_full, aa_ss, aa_rs)

    for j in range(3):
        dense_s[:, :, HF * j : HF * (j + 1)] = (
            tn(normed[...], dq_all[j]).astype(bf16).reshape(DP, MSG, HF)
        )
    dense_s[:, :, 3 * HF : D] = tn(do, call[mz]).astype(bf16).reshape(DP, MSG, HF)
    dense_s[:, :, D:] = small.astype(bf16).reshape(DP, MSG, SMALL)
    dense_s[0, :, D:] = (small[0:MSG, :] + bias_part).astype(bf16)

    @pl.when(jnp.logical_not(first))
    def _():
        hand(mz, back_ss, back_rs, in_full, gin).start()
        for i in range(1, TZ):
            gather_recv(in_full, aa_ss, aa_rs, i)
            hand(lax.rem(mz + i, TZ), back_ss, back_rs, in_full, gin).start()

    swap_start(dense_s, dense_r, dn_ss, dn_rs)

    @pl.when(first)
    def _():
        for i in range(1, TZ):
            gather_recv(in_full, aa_ss, aa_rs, i)

    grad_out[...] = in_full[...].reshape(ROWS, D)

    swap_recv_all(dense_s, dense_r, dn_ss, dn_rs)
    total = dense_r[0].astype(f32)
    for p in range(1, DP):
        total += dense_r[p].astype(f32)
    dense_f[me] = total[:, 0:D].astype(bf16)
    small_z[mz] = total[:, D:].astype(bf16)
    gather_start(small_z, sz_ss, sz_rs)

    def spread(buf, ss, rs):
        def step(i, carry):
            dp_copy(buf.at[me], buf.at[me], ss, rs, lax.rem(me + i, DP), me).start()
            return carry

        lax.fori_loop(1, DP, step, 0)

    def spread_recv(buf, ss, rs):
        def step(i, carry):
            src = lax.rem(me + DP - i, DP)
            dp_copy(buf.at[src], buf.at[src], ss, rs, src, src).wait_recv()
            return carry

        lax.fori_loop(1, DP, step, 0)

    def spread_sent(buf, ss, rs):
        def step(i, carry):
            dp_copy(buf.at[me], buf.at[me], ss, rs, lax.rem(me + i, DP), me).wait_send()
            return carry

        lax.fori_loop(1, DP, step, 0)

    spread(dense_f, df_ss, df_rs)
    for i in range(1, TZ):
        gather_recv(small_z, sz_ss, sz_rs, i)
    small_total = small_z[0].astype(f32)
    for t in range(1, TZ):
        small_total += small_z[t].astype(f32)
    small_f[me] = small_total.astype(bf16)
    spread(small_f, sf_ss, sf_rs)

    gather_sent(wall, w_ss, w_rs)
    gather_sent(call, c_ss, c_rs)
    swap_sent(send_b, recv_b, b_ss, b_rs)
    swap_sent(send_e, recv_e, e_ss, e_rs)
    swap_sent(send_d, recv_d, d_ss, d_rs)
    swap_sent(send_x, recv_x, x_ss, x_rs)
    scatter_sent(part_y, rs_y, ry_ss, ry_rs)
    gather_sent(gact, ay_ss, ay_rs)
    scatter_sent(part_h, rs_h, rh_ss, rh_rs)
    gather_sent(dh_full, ah_ss, ah_rs)
    scatter_sent(part_a, rs_a, ra_ss, ra_rs)
    gather_sent(in_full, aa_ss, aa_rs)
    swap_sent(dense_s, dense_r, dn_ss, dn_rs)
    gather_sent(small_z, sz_ss, sz_rs)

    @pl.when(first)
    def _():
        for t in range(TZ):
            hand(t, hand_ss, hand_rs, gact, xin).wait_send()

    @pl.when(jnp.logical_not(first))
    def _():
        for t in range(TZ):
            hand(t, back_ss, back_rs, in_full, gin).wait_send()

    spread_recv(dense_f, df_ss, df_rs)
    dense_out[...] = dense_f[...].reshape(D, D)
    spread_recv(small_f, sf_ss, sf_rs)
    small_out[...] = small_f[...].reshape(D, SMALL)
    spread_sent(dense_f, df_ss, df_rs)
    spread_sent(small_f, sf_ss, sf_rs)
    save_xe.wait()
    save_u.wait()
    save_de.wait()
    save_dpre.wait()


def body(
    tokens, cotangent, norm_gains, w_qkv, w_attn_out, bias_table, router, w_in, w_out, routes, segments
):
    vmem = pl.BlockSpec(memory_space=pltpu.VMEM)
    hbm = pl.BlockSpec(memory_space=pl.ANY)
    dma = pltpu.SemaphoreType.DMA
    rows3 = pltpu.VMEM((TZ, OWN, D), bf16)
    messages = pltpu.VMEM((DP, MSG, D), bf16)
    expert_rows = pltpu.VMEM((2, ER, D), bf16)
    scratch = dict(
        xin=rows3,
        gin=rows3,
        w_in=pltpu.VMEM((2, D, D), bf16),
        w_out=pltpu.VMEM((2, D, D), bf16),
        wall=pltpu.VMEM((TZ, HF, D), bf16),
        call=pltpu.VMEM((TZ, ROWS, HF), bf16),
        normed=pltpu.VMEM((ROWS, D), bf16),
        qkv=pltpu.VMEM((3, ROWS, HF), bf16),
        probs=pltpu.VMEM((2 * HEADS, BLOCK, BLOCK), f32),
        hidden=pltpu.VMEM((ROWS, D), f32),
        hid_scale=pltpu.VMEM((ROWS, 1), f32),
        normed2=pltpu.VMEM((ROWS, D), bf16),
        rpad=pltpu.VMEM((D, SMALL), bf16),
        gate=pltpu.VMEM((ROWS, 2), f32),
        slots=pltpu.VMEM((ROWS, 2), jnp.int32),
        ptg=pltpu.VMEM((ROWS, SLOTS), bf16),
        send_b=messages, recv_b=messages, send_e=messages, recv_e=messages,
        send_d=messages, recv_d=messages, send_x=messages, recv_x=messages,
        xe=expert_rows, act=expert_rows, dact=expert_rows, de=expert_rows, dpre=expert_rows,
        yf=pltpu.VMEM((2, ER, D), f32),
        part_y=rows3, rs_y=rows3, part_h=rows3, rs_h=rows3, dh_full=rows3,
        part_a=rows3, rs_a=rows3, in_full=rows3,
        dq_all=pltpu.VMEM((3, ROWS, HF), bf16),
        gact=rows3,
        dense_s=pltpu.VMEM((DP, MSG, D + SMALL), bf16),
        dense_r=pltpu.VMEM((DP, MSG, D + SMALL), bf16),
        dense_f=messages,
        small_z=pltpu.VMEM((TZ, MSG, SMALL), bf16),
        small_f=pltpu.VMEM((DP, MSG, SMALL), bf16),
        ld_sem=dma((2,)),
        out_sem=dma((4,)),
    )
    for name in ("w", "c"):
        scratch[name + "_ss"] = dma((TZ,))
        scratch[name + "_rs"] = dma((TZ,))
    for name in ("b", "e", "d", "x"):
        scratch[name + "_ss"] = dma((DP,))
        scratch[name + "_rs"] = dma((DP,))
    for name in ("ry", "ay", "rh", "ah", "ra", "aa", "hand", "back"):
        scratch[name + "_ss"] = dma((TZ,))
        scratch[name + "_rs"] = dma((TZ,))
    for name in ("dn", "df"):
        scratch[name + "_ss"] = dma((DP,))
        scratch[name + "_rs"] = dma((DP,))
    scratch["sz_ss"] = dma((TZ,))
    scratch["sz_rs"] = dma((TZ,))
    scratch["sf_ss"] = dma((DP,))
    scratch["sf_rs"] = dma((DP,))
    scratch["turn_sem"] = pltpu.SemaphoreType.REGULAR

    shape = jax.ShapeDtypeStruct
    act, grads, dense, small, xe, act_u, dpre, de = pl.pallas_call(
        kernel,
        out_shape=(
            shape((ROWS, D), bf16),
            shape((ROWS, D), bf16),
            shape((D, D), bf16),
            shape((D, SMALL), bf16),
            shape((2, ER, D), bf16),
            shape((2, ER, D), bf16),
            shape((2, ER, D), bf16),
            shape((2, ER, D), bf16),
        ),
        in_specs=[vmem] * 7 + [hbm] * 2 + [vmem] * 2,
        out_specs=(vmem,) * 4 + (hbm,) * 4,
        scratch_shapes=list(scratch.values()),
        compiler_params=pltpu.CompilerParams(
            collective_id=0, has_side_effects=True, vmem_limit_bytes=58 * 1024 * 1024
        ),
        name="layers",
    )(
        tokens, cotangent, norm_gains, w_qkv, w_attn_out, bias_table, router,
        w_in[0], w_out[0], routes, segments,
    )
    inner = jnp.einsum("erd,erf->edf", xe, dpre, preferred_element_type=f32)
    outer = jnp.einsum("erf,erd->efd", act_u, de, preferred_element_type=f32)
    dense = dense.astype(f32)
    small = small.astype(f32)
    qkv_grad = jnp.stack([dense[:, HF * j : HF * (j + 1)] for j in range(3)])
    attn_grad = dense[:, 3 * HF :].T
    gain_grad = jnp.stack([small[:, GAIN0], small[:, GAIN1]])
    bias_all = lax.dynamic_slice_in_dim(small[0:MSG], BIAS + lax.axis_index("tensor"), 1, axis=1)
    return (
        act[None],
        grads.astype(f32)[None],
        gain_grad[None],
        qkv_grad[None],
        attn_grad[None],
        bias_all.reshape(1, 16, HEADS),
        small[:, 0:32][None],
        inner[None],
        outer[None],
    )


def solution(mesh):
    in_specs = (
        P("dp", None),
        P("dp", None),
        P("section", None, None),
        P("section", None, None, "tensor"),
        P("section", "tensor", None),
        P("section", None, "tensor"),
        P("section", None, None),
        P("section", "dp", None, "tensor"),
        P("section", "dp", "tensor", None),
        P("section", "dp", None),
        P("dp", None),
    )
    out_specs = (
        P("section", "dp", None),
        P("section", "dp", None),
        P("section", None, None),
        P("section", None, None, "tensor"),
        P("section", "tensor", None),
        P("section", None, "tensor"),
        P("section", None, None),
        P("section", "dp", None, "tensor"),
        P("section", "dp", "tensor", None),
    )
    return jax.shard_map(body, mesh=mesh, in_specs=in_specs, out_specs=out_specs, check_vma=False)
```

time: 854 us -> 244 us (0.29); the launches traced: 843 us -> 244 us
  waiting for transfers between devices: 237 us -> 0 us
  blocking collectives: 234 us -> 0 us
  Pallas kernels: 0 us -> 215 us
  local copies, waits for them, and re-layouts: 111 us -> 15 us
  other arithmetic: 90.5 us -> 4.18 us
  matrix products: 85 us -> 9.05 us
  starting transfers between devices: 68.8 us -> 0 us
  between operations: 17.1 us -> 0.71 us
    psum x5 -> x0, blocking collectives: 234 us -> none  [the longest x4 158 us: settle(): summed = lax.psum(partial_value, 'tensor').astype(jnp.bfloat16)]
    pallas_call x0 -> x1, Pallas kernels: none -> 215 us  [body(): pl.pallas_call(kernel, out_shape=(shape((ROWS, D), bf16), shape((ROWS, D)...]
    psum x6 -> x0, waiting for transfers between devices: 180 us -> none  [the longest x5 180 us: heads_total(): lax.psum(partial_value.astype(jnp.bfloat16), 'tensor').astype(jnp.float32)]
    dot_general x70 -> x2, matrix products: 82.3 us -> 9.05 us  [the longest x1 5.4 us: body(): inner = jnp.einsum('erd,erf->edf', xe, dpre, preferred_element_type=f32)]
    all_to_all x12 -> x0, starting transfers between devices: 61 us -> none  [the longest x6 36.4 us: dispatch(): return lax.all_to_all(buffer, 'dp', split_axis=0, concat_axis=0, tiled=True)]
    all_to_all x12 -> x0, waiting for transfers between devices: 55.3 us -> none  [the longest x6 29.7 us: dispatch(): return lax.all_to_all(buffer, 'dp', split_axis=0, concat_axis=0, tiled=True)]
    reduce_sum x31 -> x0, other arithmetic: 33 us -> none  [the longest x3 8.48 us: expert_backward(): jnp.sum(returned_grad.astype(jnp.float32), axis=1)]
    gather x21 -> x0, local copies, waits for them, and re-layouts: 22.4 us -> none  [the longest x15 7.99 us: expert_forward(): jnp.take_along_axis(logits, route_pairs, axis=1)]
  transfers between devices with their start and end apart: 22 -> 0, of which waited for: 19 -> 0; matrix products, arithmetic and copies ran while one was open for 15% -> 0% of each run, Pallas kernels for 0% -> 0%
where the time goes in v1:
time: 244 us
  Pallas kernels  215 us (88%)
  local copies, waits for them, and re-layouts  15 us (6%)
  matrix products  9.05 us (4%)
  other arithmetic  4.18 us (2%)
    pallas_call x1, Pallas kernels, body(): pl.pallas_call(kernel, out_shape=(shape((ROWS, D), bf16), shape((ROWS, D)...  215 us
    unnamed x19, local copies, waits for them, and re-layouts  11.8 us
    dot_general x1, matrix products, body(): inner = jnp.einsum('erd,erf->edf', xe, dpre, preferred_element_type=f32)  5.4 us

profile of v1, /device:TPU:0, one launch (start us, length us, event | category | flops | bytes accessed | tf_op | source)
XLA Modules:
  0.0 243.7 jit_solution(14263488658716048554)
XLA Ops:
  0.6 1.4 copy.31.bias_tab
  2.0 1.5 copy.33.routes
  3.5 1.6 copy.32.router
  5.1 2.3 copy.30.w_qkv
  7.4 214.8 %layers.1 = (bf16[256,768]{1,0:T(8,128)(2,1)}, bf16[256,768]{1,0:T(8,128)(2,1)}, bf16[768,768]{1,0:T(8,128)(2,1)}, bf16[768,128]{1,0:T(8,128)(2,1)}, bf16[2,384,...) custom-call(bf16[256,768]{1,0:T(8,128)(2,1)} %tokens.1, ...), custom_call_target="tpu_custom_call" | custom-call | tf_op jit(solution)/shard_map/layers/pallas_call | solution.py:654
  222.2 0.7 slice.38
  222.9 0.2 dynamic-slice_reduce_fusion
  223.1 0.1 reshape.21
  223.2 0.7 copy.38
  223.8 1.0 convert_element_type.7
  224.8 0.0 copy-start.4
  224.8 0.5 slice_reduce_fusion.1
  225.3 0.0 copy-start.2
  225.4 0.8 copy.39
  226.1 0.6 maximum_bitcast_fusion.1
  226.8 0.0 copy-done.4
  226.8 0.9 bitcast_convert_fusion
  227.7 0.0 copy-done.2
  227.7 0.2 convert_element_type.8
  227.9 1.6 slice_bitcast_fusion
  229.5 1.1 copy.37
  230.6 1.5 maximum_bitcast_fusion
  232.1 1.8 copy.36
  233.9 0.0 copy-start
  233.9 0.0 copy-start.1
  233.9 5.4 %convolution_bitcast_fusion.1 = f32[1,2,768,768]{3,2,1,0:T(8,128)} fusion(bf16[2,384,768]{2,1,0:T(8,128)(2,1)} %get-tuple-element.21, bf16[2,384,768]{2,1,0:T(8,128)(2,1)} %get-tuple-element.22), kind=kOutput, calls=%fused_computation.2 | convolution fusion | flops 905969664 | bytes 7077888 | tf_op jit(solution)/shard_map/erd,erf->edf/dot_general | solution.py:677
  239.3 0.0 copy-done
  239.3 0.0 copy-done.1
  239.3 0.0 copy-start.3
  239.3 3.7 %convolution_bitcast_fusion = f32[1,2,768,768]{3,2,1,0:T(8,128)} fusion(bf16[2,384,768]{2,1,0:T(8,128)(2,1)S(1)} %copy-done, bf16[2,384,768]{2,1,0:T(8,128)(2,1)S(1)} %copy-done.1), kind=kOutput, calls=%fused_computation.1 | convolution fusion | flops 905969664 | bytes 7077888 | tf_op jit(solution)/shard_map/erf,erd->efd/dot_general | solution.py:678
  243.0 0.0 copy-done.3
  243.0 0.7 copy.43
  (3 shorter events, 0.0 us)
Async XLA Ops:
  224.8 2.0 copy-start.4
  225.3 2.4 copy-start.2
  233.9 5.4 %copy-start = (bf16[2,384,768]{2,1,0:T(8,128)(2,1)S(1)}, bf16[2,384,768]{2,1,0:T(8,128)(2,1)}, u32[]{:S(2)}) copy-start(bf16[2,384,768]{2,1,0:T(8,128)(2,1)} %get-tuple-element.23) | copy-start | bytes 3538948
  233.9 5.4 %copy-start.1 = (bf16[2,384,768]{2,1,0:T(8,128)(2,1)S(1)}, bf16[2,384,768]{2,1,0:T(8,128)(2,1)}, u32[]{:S(2)}) copy-start(bf16[2,384,768]{2,1,0:T(8,128)(2,1)} %get-tuple-element.24) | copy-start | bytes 3538948
  239.3 3.7 %copy-start.3 = (bf16[256,768]{1,0:T(8,128)(2,1)S(1)}, bf16[256,768]{1,0:T(8,128)(2,1)}, u32[]{:S(2)}) copy-start(bf16[256,768]{1,0:T(8,128)(2,1)} %get-tuple-element.17) | copy-start | bytes 1179652

commit v2 on v1

v2 whole, which is shorter than its diff:
```python
import jax
import jax.numpy as jnp
from jax import lax
from jax.experimental import pallas as pl
from jax.experimental.pallas import tpu as pltpu
from jax.sharding import PartitionSpec as P

epsilon = 1e-06
masked_score = -1000000000.0
bucket_edges = (1, 2, 3, 4, 5, 6, 7, 8, 10, 13, 16, 20, 25, 32, 40)
MESH = pl.DeviceIdType.MESH
f32 = jnp.float32
bf16 = jnp.bfloat16

DP = 16
TZ = 4
ROWS = 256
BLOCK = 128
OWN = BLOCK // TZ
D = 768
HF = 192
HEADS = 3
PAD = 16
ER = DP * PAD
SLOTS = 2 * ER
WIDE = D + 128
CUT = D // DP
SMALL = 48
GAIN0, GAIN1, BIAS = 32, 33, 34
HALF = D // 2
PARTS = D // 128
EDGES = (0,) + bucket_edges


def nn(a, b):
    return lax.dot_general(a, b, (((1,), (0,)), ((), ())), preferred_element_type=f32)


def nt(a, b):
    return lax.dot_general(a, b, (((1,), (1,)), ((), ())), preferred_element_type=f32)


def tn(a, b):
    return lax.dot_general(a, b, (((0,), (0,)), ((), ())), preferred_element_type=f32)


def iota(shape, dim):
    return lax.broadcasted_iota(jnp.int32, shape, dim)


def rms_scale(values):
    return lax.rsqrt(jnp.mean(values * values, axis=-1, keepdims=True) + epsilon)


def kernel(
    tokens, cotangent, gains, w_qkv, w_att, bias_tab, router, w_in_hbm, w_out_hbm, routes, segments,
    act_out, grad_out, dense_out, small_out, xe_out, u_out, dpre_out, de_out,
    xin, gin, w_in, w_out, wall, call, normed, qkv, probs, hidden, hid_scale, normed2, rpad,
    gate, slots, hits, ptg, pick, pick_g, send_b, recv_b, send_e, recv_e, send_d, recv_d, send_x,
    recv_x, act, dact, dpre, part_y, rs_y, part_h, rs_h, dh_own, dh_full, part_a, rs_a, in_full,
    dq_all, score_sum, gact, dense_s, dense_r, dense_f, small_acc, small_s, small_r, small_z, small_f,
    ld_sem, out_sem, w_ss, w_rs, c_ss, c_rs, b_ss, b_rs, e_ss, e_rs, d_ss, d_rs, x_ss, x_rs,
    ry_ss, ry_rs, ay_ss, ay_rs, rh_ss, rh_rs, ah_ss, ah_rs, ra_ss, ra_rs, aa_ss, aa_rs,
    hand_ss, hand_rs, back_ss, back_rs, dn_ss, dn_rs, df_ss, df_rs, sm_ss, sm_rs, sz_ss, sz_rs,
    sf_ss, sf_rs, turn_sem,
):
    sec = lax.axis_index("section")
    me = lax.axis_index("dp")
    mz = lax.axis_index("tensor")
    first = sec == 0
    second = sec == 1

    load_in = pltpu.make_async_copy(w_in_hbm, w_in, ld_sem.at[0])
    load_out = pltpu.make_async_copy(w_out_hbm, w_out, ld_sem.at[1])
    load_in.start()
    load_out.start()

    barrier = pltpu.get_barrier_semaphore()

    def greet(i, carry):
        pl.semaphore_signal(
            barrier, inc=1, device_id={"dp": lax.rem(me + i, DP)}, device_id_type=MESH
        )
        return carry

    lax.fori_loop(1, DP, greet, 0)
    for i in range(1, TZ):
        pl.semaphore_signal(
            barrier, inc=1, device_id={"tensor": lax.rem(mz + i, TZ)}, device_id_type=MESH
        )
    pl.semaphore_signal(barrier, inc=1, device_id={"section": 1 - sec}, device_id_type=MESH)

    def z_copy(src, dst, ss, rs, peer, slot):
        return pltpu.make_async_remote_copy(
            src_ref=src, dst_ref=dst, send_sem=ss.at[peer], recv_sem=rs.at[slot],
            device_id={"tensor": peer}, device_id_type=MESH,
        )

    def gather_start(buf, ss, rs):
        for i in range(1, TZ):
            z_copy(buf.at[mz], buf.at[mz], ss, rs, lax.rem(mz + i, TZ), mz).start()

    def gather_recv(buf, ss, rs, i):
        src = lax.rem(mz + i, TZ)
        z_copy(buf.at[src], buf.at[src], ss, rs, src, src).wait_recv()

    def gather_sent(buf, ss, rs):
        for i in range(1, TZ):
            z_copy(buf.at[mz], buf.at[mz], ss, rs, lax.rem(mz + i, TZ), mz).wait_send()

    def scatter_start(part, rcv, ss, rs):
        for i in range(1, TZ):
            peer = lax.rem(mz + i, TZ)
            z_copy(part.at[peer], rcv.at[mz], ss, rs, peer, mz).start()

    def scatter_sum(part, rcv, ss, rs):
        total = part[mz].astype(f32)
        for i in range(1, TZ):
            src = lax.rem(mz + i, TZ)
            z_copy(part.at[src], rcv.at[src], ss, rs, src, src).wait_recv()
            total += rcv[src].astype(f32)
        return total

    def scatter_sent(part, rcv, ss, rs):
        for i in range(1, TZ):
            peer = lax.rem(mz + i, TZ)
            z_copy(part.at[peer], rcv.at[mz], ss, rs, peer, mz).wait_send()

    def dp_copy(src, dst, ss, rs, peer, slot):
        return pltpu.make_async_remote_copy(
            src_ref=src, dst_ref=dst, send_sem=ss.at[peer], recv_sem=rs.at[slot],
            device_id={"dp": peer}, device_id_type=MESH,
        )

    def others(step):
        def one(i, carry):
            step(lax.rem(me + i, DP))
            return carry

        lax.fori_loop(1, DP, one, 0)

    def others_back(step):
        def one(i, carry):
            step(lax.rem(me + DP - i, DP))
            return carry

        lax.fori_loop(1, DP, one, 0)

    def swap_start(snd, rcv, ss, rs):
        others(lambda peer: dp_copy(snd.at[peer], rcv.at[me], ss, rs, peer, me).start())
        rcv[me] = snd[me]

    def swap_recv(snd, rcv, ss, rs):
        others_back(lambda src: dp_copy(snd.at[src], rcv.at[src], ss, rs, src, src).wait_recv())

    def swap_sent(snd, rcv, ss, rs):
        others(lambda peer: dp_copy(snd.at[peer], rcv.at[me], ss, rs, peer, me).wait_send())

    def spread(buf, ss, rs):
        others(lambda peer: dp_copy(buf.at[me], buf.at[me], ss, rs, peer, me).start())

    def spread_recv(buf, ss, rs):
        others_back(lambda src: dp_copy(buf.at[src], buf.at[src], ss, rs, src, src).wait_recv())

    def spread_sent(buf, ss, rs):
        others(lambda peer: dp_copy(buf.at[me], buf.at[me], ss, rs, peer, me).wait_send())

    def hand(b, t, ss, rs, src, dst):
        return pltpu.make_async_remote_copy(
            src_ref=src.at[b, t], dst_ref=dst.at[b, t], send_sem=ss.at[b, t],
            recv_sem=rs.at[b, t], device_id={"section": 1 - sec}, device_id_type=MESH,
        )

    def both(sems, b):
        return sems[0].at[b], sems[1].at[b]

    c_sem, b_sem, d_sem = (c_ss, c_rs), (b_ss, b_rs), (d_ss, d_rs)
    ry, ay, rh = (ry_ss, ry_rs), (ay_ss, ay_rs), (rh_ss, rh_rs)
    ah, ra, aa = (ah_ss, ah_rs), (ra_ss, ra_rs), (aa_ss, aa_rs)
    dn, df = (dn_ss, dn_rs), (df_ss, df_rs)

    row = iota((BLOCK, BLOCK), 0)
    col = iota((BLOCK, BLOCK), 1)
    eye = row == col
    earlier = (row > col).astype(f32).astype(bf16)
    every = jnp.ones((BLOCK, BLOCK), bf16)
    lane = iota((BLOCK, SMALL), 1)
    slot_lane = iota((BLOCK, SLOTS), 1)
    slot_sub = iota((SLOTS, BLOCK), 0)

    def to_col(values):
        return jnp.sum(jnp.where(eye, values, 0.0), axis=1, keepdims=True)

    def to_row(values):
        return jnp.sum(jnp.where(eye, values, 0.0), axis=0, keepdims=True)

    rpad[...] = jnp.zeros((SMALL, D), bf16)
    rpad[0:32, :] = router[0]
    for b in range(2):
        named = routes[0, :, b * BLOCK : (b + 1) * BLOCK].astype(f32)
        e0 = to_col(named[0:1, :]).astype(jnp.int32)
        e1 = to_col(named[1:2, :]).astype(jnp.int32)
        hit0 = (lane == e0).astype(f32)
        hit1 = (lane == e1).astype(f32)
        rank0 = jnp.sum(nn(earlier, hit0.astype(bf16)) * hit0, axis=1, keepdims=True)
        rank1 = jnp.sum(
            (nn(earlier, hit1.astype(bf16)) + nn(every, hit0.astype(bf16))) * hit1,
            axis=1, keepdims=True,
        )
        slot0 = (e0 % 2) * ER + (e0 // 2) * PAD + rank0.astype(jnp.int32)
        slot1 = (e1 % 2) * ER + (e1 // 2) * PAD + rank1.astype(jnp.int32)
        slots[b, :, 0:1] = slot0
        slots[b, :, 1:2] = slot1
        hits[b, 0] = hit0
        hits[b, 1] = hit1
        row0 = to_row(slot0.astype(f32)).astype(jnp.int32)
        row1 = to_row(slot1.astype(f32)).astype(jnp.int32)
        pick[b] = ((slot_sub == row0) | (slot_sub == row1)).astype(f32).astype(bf16)

    @pl.when(first)
    def _():
        xin[...] = tokens[...].reshape(2, TZ, OWN, D)

    @pl.when(second)
    def _():
        gin[...] = cotangent[...].reshape(2, TZ, OWN, D)

    wall[mz] = w_att[0]
    gain0 = gains[0, 0:1, :].astype(f32)
    gain1 = gains[0, 1:2, :].astype(f32)
    gap = row - col
    head_of = iota((BLOCK, HF), 1) // (HF // HEADS)

    pl.semaphore_wait(barrier, DP + TZ - 1)

    @pl.when(second)
    def _():
        pl.semaphore_wait(turn_sem, 1)

    gather_start(wall, w_ss, w_rs)

    for b in range(2):
        rows = slice(b * BLOCK, (b + 1) * BLOCK)

        @pl.when(second)
        def _():
            for t in range(TZ):
                hand(b, t, hand_ss, hand_rs, gact, xin).wait_recv()

        x = xin[b].reshape(BLOCK, D).astype(f32)
        normed[rows, :] = (x * rms_scale(x) * gain0).astype(bf16)
        for j in range(3):
            qkv[j, rows, :] = nt(normed[rows, :], w_qkv[0, j]).astype(bf16)
        seg_row = segments[b : b + 1, :].astype(f32)
        allowed = (gap >= 0) & (seg_row == to_col(seg_row))
        q = qkv[0, rows, :]
        k = qkv[1, rows, :]
        v = qkv[2, rows, :]
        context = jnp.zeros((BLOCK, HF), f32)
        for h in range(HEADS):
            bias = jnp.broadcast_to(bias_tab[0, h : h + 1, 0:1].astype(f32), (BLOCK, BLOCK))
            for n, edge in enumerate(bucket_edges):
                bias = jnp.where(
                    gap >= edge, bias_tab[0, h : h + 1, n + 1 : n + 2].astype(f32), bias
                )
            score = nt(jnp.where(head_of == h, q, jnp.zeros_like(q)), k) * 0.125 + bias
            score = jnp.where(allowed, score, masked_score)
            score = jnp.exp(score - jnp.max(score, axis=-1, keepdims=True))
            prob = score / jnp.sum(score, axis=-1, keepdims=True)
            probs[b * HEADS + h] = prob
            context = jnp.where(head_of == h, nn(prob.astype(bf16), v), context)
        call[b, mz] = context.astype(bf16)
        gather_start(call.at[b], *both(c_sem, b))

    def dispatch(chosen, values, snd, rcv, sems, b):
        for e in range(2):
            out = nn(chosen[b, ER * e : ER * (e + 1), :], values).astype(bf16)
            snd[b, e] = out.reshape(DP, PAD, D)
            swap_start(snd.at[b, e], rcv.at[b, e], sems[0].at[b, e], sems[1].at[b, e])

    def dispatch_grad(b):
        dispatch(pick_g, gin[b].reshape(BLOCK, D), send_d, recv_d, d_sem, b)

    for b in range(2):
        for i in range(1, TZ):
            gather_recv(call.at[b], *both(c_sem, b), i)
        if b == 0:
            for i in range(1, TZ):
                gather_recv(wall, w_ss, w_rs, i)

            @pl.when(first)
            def _():
                pl.semaphore_signal(
                    turn_sem, inc=1, device_id={"section": 1 - sec}, device_id_type=MESH
                )

        h = xin[b].reshape(BLOCK, D).astype(f32)
        for t in range(TZ):
            h += nn(call[b, t], wall[t])
        hidden[b] = h
        scale = rms_scale(h)
        hid_scale[b] = scale
        normed2[b] = (h * scale * gain1).astype(bf16)
        dispatch(pick, normed2[b], send_b, recv_b, b_sem, b)

        z = nt(normed2[b], rpad[...])
        z0 = jnp.sum(z * hits[b, 0], axis=1, keepdims=True)
        z1 = jnp.sum(z * hits[b, 1], axis=1, keepdims=True)
        g0 = 1.0 / (1.0 + jnp.exp(z1 - z0))
        g1 = 1.0 / (1.0 + jnp.exp(z0 - z1))
        gate[b, :, 0:1] = g0
        gate[b, :, 1:2] = g1
        slot0 = slots[b, :, 0:1]
        slot1 = slots[b, :, 1:2]
        row0 = to_row(slot0.astype(f32)).astype(jnp.int32)
        row1 = to_row(slot1.astype(f32)).astype(jnp.int32)
        pick_g[b] = (
            jnp.where(slot_sub == row0, to_row(g0), 0.0)
            + jnp.where(slot_sub == row1, to_row(g1), 0.0)
        ).astype(bf16)

        @pl.when(second)
        def _():
            dispatch_grad(b)

        ptg[b] = (
            jnp.where(slot_lane == slot0, g0, 0.0) + jnp.where(slot_lane == slot1, g1, 0.0)
        ).astype(bf16)

    root = 0.7978845608028654
    saved = []

    def save(b, n, src, dst):
        copy = pltpu.make_async_copy(src.at[b], dst.at[b], out_sem.at[b, n])
        copy.start()
        saved.append(copy)

    def expert_forward(b, e):
        swap_recv(send_b.at[b, e], recv_b.at[b, e], b_ss.at[b, e], b_rs.at[b, e])
        x = recv_b[b, e].reshape(ER, D)
        for n in range(3):
            cols = slice(256 * n, 256 * (n + 1))
            pre = nn(x, w_in[e, :, cols])
            square = pre * pre
            wave = jnp.tanh(root * pre * (1.0 + 0.044715 * square))
            lift = 0.5 * (1.0 + wave)
            act[b, e, :, cols] = (pre * lift).astype(bf16)
            slope = lift + 0.5 * root * pre * (1.0 - wave * wave) * (1.0 + 0.134145 * square)
            dact[b, e, :, cols] = slope.astype(bf16)
        out = nn(act[b, e], w_out[e])
        send_e[b, e] = out.astype(bf16).reshape(DP, PAD, D)

    def return_rows(b, e):
        swap_start(send_e.at[b, e], recv_e.at[b, e], e_ss.at[b, e], e_rs.at[b, e])

    def expert_backward(b, e):
        swap_recv(send_d.at[b, e], recv_d.at[b, e], d_ss.at[b, e], d_rs.at[b, e])
        de = recv_d[b, e].reshape(ER, D)
        for n in range(3):
            cols = slice(256 * n, 256 * (n + 1))
            grad = nt(de, w_out[e, cols, :])
            dpre[b, e, :, cols] = (grad * dact[b, e, :, cols].astype(f32)).astype(bf16)
        out = nt(dpre[b, e], w_in[e])
        send_x[b, e, :, :, 0:D] = out.astype(bf16).reshape(DP, PAD, D)
        rows = send_e[b, e].reshape(ER, D).astype(f32)
        weight = jnp.sum(rows * de.astype(f32), axis=1, keepdims=True)
        coarse = weight.astype(bf16).astype(f32)
        place = iota((ER, 128), 1)
        pair = jnp.where(place == 0, coarse, jnp.where(place == 1, weight - coarse, 0.0))
        send_x[b, e, :, :, D:] = pair.astype(bf16).reshape(DP, PAD, 128)
        swap_start(send_x.at[b, e], recv_x.at[b, e], x_ss.at[b, e], x_rs.at[b, e])

    def each_expert(step):
        def one(e, carry):
            step(e)
            return carry

        lax.fori_loop(0, 2, one, 0)

    def each_part(step):
        def one(i, carry):
            step(i // 2, i % 2)
            return carry

        lax.fori_loop(0, 4, one, 0)

    def combine(b):
        for e in range(2):
            swap_recv(send_e.at[b, e], recv_e.at[b, e], e_ss.at[b, e], e_rs.at[b, e])
        out = nn(ptg[b], recv_e[b].reshape(SLOTS, D))
        part_y[b] = out.astype(bf16).reshape(TZ, OWN, D)
        scatter_start(part_y.at[b], rs_y.at[b], *both(ry, b))

    def settle(b):
        own = pl.ds(pl.multiple_of(mz * OWN, OWN), OWN)
        total = scatter_sum(part_y.at[b], rs_y.at[b], *both(ry, b)) + hidden[b, own, :]
        gact[b, mz] = total.astype(bf16)
        gather_start(gact.at[b], *both(ay, b))

    load_in.wait()
    load_out.wait()

    @pl.when(first)
    def _():
        def part(b, e):
            expert_forward(b, e)
            return_rows(b, e)

        each_part(part)

    @pl.when(second)
    def _():
        def block(b, carry):
            each_expert(lambda e: expert_forward(b, e))
            each_expert(lambda e: expert_backward(b, e))
            return carry

        lax.fori_loop(0, 2, block, 0)
        each_part(return_rows)

    for b in range(2):
        save(b, 0, recv_b, xe_out)
        save(b, 1, act, u_out)

    @pl.when(first)
    def _():
        combine(0)
        combine(1)
        for b in range(2):
            settle(b)
            hand(b, mz, hand_ss, hand_rs, gact, xin).start()
        for b in range(2):
            for i in range(1, TZ):
                gather_recv(gact.at[b], *both(ay, b), i)
                hand(b, lax.rem(mz + i, TZ), hand_ss, hand_rs, gact, xin).start()
        for b in range(2):
            for t in range(TZ):
                hand(b, t, back_ss, back_rs, in_full, gin).wait_recv()
            dispatch_grad(b)
        each_part(expert_backward)

    for b in range(2):
        save(b, 2, recv_d, de_out)
        save(b, 3, dpre, dpre_out)

    for b in range(2):
        pt0 = (slot_lane == slots[b, :, 0:1]).astype(f32).astype(bf16)
        pt1 = (slot_lane == slots[b, :, 1:2]).astype(f32).astype(bf16)
        for e in range(2):
            swap_recv(send_x.at[b, e], recv_x.at[b, e], x_ss.at[b, e], x_rs.at[b, e])
        back = recv_x[b].reshape(SLOTS, WIDE)
        q0 = jnp.sum(nn(pt0, back[:, D:]), axis=1, keepdims=True)
        q1 = jnp.sum(nn(pt1, back[:, D:]), axis=1, keepdims=True)
        dc = gate[b, :, 1:2] * q0 - gate[b, :, 0:1] * q1
        dz = ((hits[b, 0] - hits[b, 1]) * dc).astype(bf16)
        db = nn(pt0 + pt1, back[:, 0:D]) + nn(dz, rpad[...])
        part_h[b] = db.astype(bf16).reshape(TZ, OWN, D)
        scatter_start(part_h.at[b], rs_h.at[b], *both(rh, b))
        unit = (lane == GAIN1).astype(f32).astype(bf16)
        small = tn(dz, normed2[b])
        small += tn(unit, (db * hidden[b] * hid_scale[b]).astype(bf16))
        if b == 0:
            small_acc[...] = small
        else:
            small_acc[...] += small

    for b in range(2):
        own = pl.ds(pl.multiple_of(mz * OWN, OWN), OWN)
        s_own = hid_scale[b, own, :]
        hat = hidden[b, own, :] * s_own
        lifted = scatter_sum(part_h.at[b], rs_h.at[b], *both(rh, b)) * gain1
        total = gin[b, mz].astype(f32) + s_own * (
            lifted - hat * jnp.mean(lifted * hat, axis=-1, keepdims=True)
        )
        dh_own[b] = total
        dh_full[b, mz] = total.astype(bf16)
        gather_start(dh_full.at[b], *both(ah, b))

    for b in range(2):
        rows = slice(b * BLOCK, (b + 1) * BLOCK)
        for i in range(1, TZ):
            gather_recv(dh_full.at[b], *both(ah, b), i)
        dc = nt(dh_full[b].reshape(BLOCK, D), w_att[0]).astype(bf16)
        q = qkv[0, rows, :]
        k = qkv[1, rows, :]
        v = qkv[2, rows, :]
        dq = jnp.zeros((BLOCK, HF), f32)
        dk = jnp.zeros((BLOCK, HF), f32)
        dv = jnp.zeros((BLOCK, HF), f32)
        for h in range(HEADS):
            mine = head_of == h
            prob = probs[b * HEADS + h]
            dp = nt(jnp.where(mine, dc, jnp.zeros_like(dc)), v)
            ds = (prob * (dp - jnp.sum(prob * dp, axis=-1, keepdims=True))).astype(bf16)
            if b == 0:
                score_sum[h] = ds.astype(f32)
            else:
                score_sum[h] += ds.astype(f32)
            dq = jnp.where(mine, nn(ds, k), dq)
            dk = jnp.where(mine, tn(ds, q), dk)
            dv = jnp.where(mine, tn(prob.astype(bf16), dc), dv)
        dq_all[0, rows, :] = (dq * 0.125).astype(bf16)
        dq_all[1, rows, :] = (dk * 0.125).astype(bf16)
        dq_all[2, rows, :] = dv.astype(bf16)
        da = nn(dq_all[0, rows, :], w_qkv[0, 0])
        da += nn(dq_all[1, rows, :], w_qkv[0, 1])
        da += nn(dq_all[2, rows, :], w_qkv[0, 2])
        part_a[b] = da.astype(bf16).reshape(TZ, OWN, D)
        scatter_start(part_a.at[b], rs_a.at[b], *both(ra, b))

    def dense_part():
        own_context = jnp.concatenate([call[0, mz], call[1, mz]], axis=0)
        for n in range(2):
            cols = slice(HALF * n, HALF * (n + 1))
            for j in range(3):
                out = tn(dq_all[j], normed[:, cols]).astype(bf16)
                dense_s[n, 4 * j : 4 * j + 4] = out.reshape(4, CUT, HALF)
            grad = dh_full[:, :, :, cols].reshape(ROWS, HALF)
            dense_s[n, 12:16] = tn(own_context, grad).astype(bf16).reshape(4, CUT, HALF)
            swap_start(dense_s.at[n], dense_r.at[n], *both(dn, n))
        small = small_acc[...]
        unit = (lane == GAIN0).astype(f32).astype(bf16)
        for b in range(2):
            x = xin[b].reshape(BLOCK, D).astype(f32)
            da = part_a[b].reshape(BLOCK, D).astype(f32)
            small += tn(unit, (da * x * rms_scale(x)).astype(bf16))
        bias_rows = []
        for h in range(HEADS):
            for n in range(len(EDGES)):
                hit = gap >= EDGES[n]
                if n + 1 < len(EDGES):
                    hit = hit & (gap < EDGES[n + 1])
                bias_rows.append(jnp.sum(jnp.where(hit, score_sum[h], 0.0), axis=0, keepdims=True))
        bias_col = jnp.sum(jnp.concatenate(bias_rows, axis=0), axis=1, keepdims=True)
        diagonal = iota((SMALL, 128), 0) == iota((SMALL, 128), 1)
        bias_row = jnp.sum(jnp.where(diagonal, bias_col, 0.0), axis=0, keepdims=True)
        mine = iota((SMALL, 128), 0) == BIAS + mz
        for j in range(PARTS):
            piece = small[:, 128 * j : 128 * (j + 1)]
            if j == 0:
                piece += jnp.where(mine, bias_row, 0.0)
            small_s[j] = piece.astype(bf16)

            @pl.when(me != j)
            def _():
                dp_copy(small_s.at[j], small_r.at[me], sm_ss, sm_rs, j, me).start()

    @pl.when(first)
    def _():
        dense_part()

    for b in range(2):
        x_own = xin[b, mz].astype(f32)
        r_own = rms_scale(x_own)
        hat = x_own * r_own
        lifted = scatter_sum(part_a.at[b], rs_a.at[b], *both(ra, b)) * gain0
        total = dh_own[b] + r_own * (lifted - hat * jnp.mean(lifted * hat, axis=-1, keepdims=True))
        in_full[b, mz] = total.astype(bf16)
        gather_start(in_full.at[b], *both(aa, b))

        @pl.when(second)
        def _():
            hand(b, mz, back_ss, back_rs, in_full, gin).start()

    for b in range(2):
        for i in range(1, TZ):
            gather_recv(in_full.at[b], *both(aa, b), i)

            @pl.when(second)
            def _():
                hand(b, lax.rem(mz + i, TZ), back_ss, back_rs, in_full, gin).start()

    grad_out[...] = in_full[...].reshape(ROWS, D)

    @pl.when(second)
    def _():
        dense_part()
        for b in range(2):
            combine(b)
        for b in range(2):
            settle(b)
        for b in range(2):
            for i in range(1, TZ):
                gather_recv(gact.at[b], *both(ay, b), i)

    act_out[...] = gact[...].reshape(ROWS, D)

    holds = me < PARTS

    for n in range(2):
        swap_recv(dense_s.at[n], dense_r.at[n], *both(dn, n))
        total = dense_r[n, 0].astype(f32)
        for p in range(1, DP):
            total += dense_r[n, p].astype(f32)
        dense_f[n, me] = total.astype(bf16)
        spread(dense_f.at[n], *both(df, n))

    @pl.when(holds)
    def _():
        small_r[me] = small_s[me]
        others_back(
            lambda src: dp_copy(small_s.at[src], small_r.at[src], sm_ss, sm_rs, src, src).wait_recv()
        )
        total = small_r[0].astype(f32)
        for p in range(1, DP):
            total += small_r[p].astype(f32)
        small_z[mz] = total.astype(bf16)
        gather_start(small_z, sz_ss, sz_rs)
        for i in range(1, TZ):
            gather_recv(small_z, sz_ss, sz_rs, i)
        total = small_z[0].astype(f32)
        for t in range(1, TZ):
            total += small_z[t].astype(f32)
        small_f[me] = total.astype(bf16)
        spread(small_f, sf_ss, sf_rs)

    gather_sent(wall, w_ss, w_rs)
    for b in range(2):
        gather_sent(call.at[b], *both(c_sem, b))
        for e in range(2):
            swap_sent(send_b.at[b, e], recv_b.at[b, e], b_ss.at[b, e], b_rs.at[b, e])
            swap_sent(send_e.at[b, e], recv_e.at[b, e], e_ss.at[b, e], e_rs.at[b, e])
            swap_sent(send_d.at[b, e], recv_d.at[b, e], d_ss.at[b, e], d_rs.at[b, e])
            swap_sent(send_x.at[b, e], recv_x.at[b, e], x_ss.at[b, e], x_rs.at[b, e])
        scatter_sent(part_y.at[b], rs_y.at[b], *both(ry, b))
        gather_sent(gact.at[b], *both(ay, b))
        scatter_sent(part_h.at[b], rs_h.at[b], *both(rh, b))
        gather_sent(dh_full.at[b], *both(ah, b))
        scatter_sent(part_a.at[b], rs_a.at[b], *both(ra, b))
        gather_sent(in_full.at[b], *both(aa, b))

        @pl.when(first)
        def _():
            for t in range(TZ):
                hand(b, t, hand_ss, hand_rs, gact, xin).wait_send()

        @pl.when(second)
        def _():
            for t in range(TZ):
                hand(b, t, back_ss, back_rs, in_full, gin).wait_send()

    for n in range(2):
        swap_sent(dense_s.at[n], dense_r.at[n], *both(dn, n))
    for j in range(PARTS):
        @pl.when(me != j)
        def _():
            dp_copy(small_s.at[j], small_r.at[me], sm_ss, sm_rs, j, me).wait_send()

    @pl.when(holds)
    def _():
        gather_sent(small_z, sz_ss, sz_rs)
        spread_sent(small_f, sf_ss, sf_rs)

    for copy in saved:
        copy.wait()
    for n in range(2):
        spread_recv(dense_f.at[n], *both(df, n))
        dense_out[:, HALF * n : HALF * (n + 1)] = dense_f[n].reshape(D, HALF)
    for j in range(PARTS):
        @pl.when(me != j)
        def _():
            dp_copy(small_f.at[j], small_f.at[j], sf_ss, sf_rs, j, j).wait_recv()

        small_out[:, 128 * j : 128 * (j + 1)] = small_f[j].astype(f32)
    held = small_f[0].astype(f32)
    mine = iota((SMALL, 128), 0) == BIAS + mz
    small_out[BIAS : BIAS + 1, 0:128] = jnp.sum(jnp.where(mine, held, 0.0), axis=0, keepdims=True)
    for n in range(2):
        spread_sent(dense_f.at[n], *both(df, n))


def last_outputs(
    xe, dpre, u, de, act, grads, dense, small,
    inner, outer, act_out, grads_out, qkv_out, attn_out, gain_out, router_out, bias_out,
):
    inner[0] = tn(xe[...].reshape(SLOTS, 256), dpre[...].reshape(SLOTS, D))
    outer[0] = tn(u[...].reshape(SLOTS, 256), de[...].reshape(SLOTS, D))
    act_out[...] = act[...]
    grads_out[...] = grads[...].astype(f32)
    qkv_out[...] = dense[0 : 3 * HF, :].astype(f32).reshape(3, HF, 128)
    attn_out[...] = dense[3 * HF :, :].astype(f32)
    router_out[...] = small[0:32, :]
    gain_out[...] = small[GAIN0 : GAIN1 + 1, :]

    @pl.when((pl.program_id(0) == 0) & (pl.program_id(1) == 0))
    def _():
        for h in range(HEADS):
            bias_out[h] = small[BIAS : BIAS + 1, 16 * h : 16 * (h + 1)]


def body(
    tokens, cotangent, norm_gains, w_qkv, w_attn_out, bias_table, router, w_in, w_out, routes, segments
):
    vmem = pl.BlockSpec(memory_space=pltpu.VMEM)
    hbm = pl.BlockSpec(memory_space=pl.ANY)
    dma = pltpu.SemaphoreType.DMA
    rows4 = pltpu.VMEM((2, TZ, OWN, D), bf16)
    messages = pltpu.VMEM((2, 2, DP, PAD, D), bf16)
    wide = pltpu.VMEM((2, 2, DP, PAD, WIDE), bf16)
    expert_rows = pltpu.VMEM((2, 2, ER, D), bf16)
    cuts = pltpu.VMEM((2, DP, CUT, HALF), bf16)
    pieces = pltpu.VMEM((DP, SMALL, 128), bf16)
    scratch = dict(
        xin=rows4,
        gin=rows4,
        w_in=pltpu.VMEM((2, D, D), bf16),
        w_out=pltpu.VMEM((2, D, D), bf16),
        wall=pltpu.VMEM((TZ, HF, D), bf16),
        call=pltpu.VMEM((2, TZ, BLOCK, HF), bf16),
        normed=pltpu.VMEM((ROWS, D), bf16),
        qkv=pltpu.VMEM((3, ROWS, HF), bf16),
        probs=pltpu.VMEM((2 * HEADS, BLOCK, BLOCK), f32),
        hidden=pltpu.VMEM((2, BLOCK, D), f32),
        hid_scale=pltpu.VMEM((2, BLOCK, 1), f32),
        normed2=pltpu.VMEM((2, BLOCK, D), bf16),
        rpad=pltpu.VMEM((SMALL, D), bf16),
        gate=pltpu.VMEM((2, BLOCK, 2), f32),
        slots=pltpu.VMEM((2, BLOCK, 2), jnp.int32),
        hits=pltpu.VMEM((2, 2, BLOCK, SMALL), f32),
        ptg=pltpu.VMEM((2, BLOCK, SLOTS), bf16),
        pick=pltpu.VMEM((2, SLOTS, BLOCK), bf16),
        pick_g=pltpu.VMEM((2, SLOTS, BLOCK), bf16),
        send_b=messages, recv_b=messages, send_e=messages, recv_e=messages,
        send_d=messages, recv_d=messages, send_x=wide, recv_x=wide,
        act=expert_rows, dact=expert_rows, dpre=expert_rows,
        part_y=rows4, rs_y=rows4, part_h=rows4, rs_h=rows4,
        dh_own=pltpu.VMEM((2, OWN, D), f32),
        dh_full=rows4, part_a=rows4, rs_a=rows4, in_full=rows4,
        dq_all=pltpu.VMEM((3, ROWS, HF), bf16),
        score_sum=pltpu.VMEM((HEADS, BLOCK, BLOCK), f32),
        gact=rows4,
        dense_s=cuts, dense_r=cuts, dense_f=cuts,
        small_acc=pltpu.VMEM((SMALL, D), f32),
        small_s=pieces, small_r=pieces,
        small_z=pltpu.VMEM((TZ, SMALL, 128), bf16),
        small_f=pieces,
        ld_sem=dma((2,)),
        out_sem=dma((2, 4)),
        w_ss=dma((TZ,)), w_rs=dma((TZ,)),
        c_ss=dma((2, TZ)), c_rs=dma((2, TZ)),
    )
    for name in ("b", "e", "d", "x"):
        scratch[name + "_ss"] = dma((2, 2, DP))
        scratch[name + "_rs"] = dma((2, 2, DP))
    for name in ("ry", "ay", "rh", "ah", "ra", "aa", "hand", "back"):
        scratch[name + "_ss"] = dma((2, TZ))
        scratch[name + "_rs"] = dma((2, TZ))
    for name in ("dn", "df"):
        scratch[name + "_ss"] = dma((2, DP))
        scratch[name + "_rs"] = dma((2, DP))
    for name, count in (("sm", DP), ("sz", TZ), ("sf", DP)):
        scratch[name + "_ss"] = dma((count,))
        scratch[name + "_rs"] = dma((count,))
    scratch["turn_sem"] = pltpu.SemaphoreType.REGULAR

    shape = jax.ShapeDtypeStruct
    rows = shape((2, 2, DP, PAD, D), bf16)
    kept = shape((2, 2, ER, D), bf16)
    act, grads, dense, small, xe, u, dpre, de = pl.pallas_call(
        kernel,
        out_shape=(
            shape((ROWS, D), bf16),
            shape((ROWS, D), bf16),
            shape((D, D), bf16),
            shape((SMALL, D), f32),
            rows, kept, kept, rows,
        ),
        in_specs=[vmem] * 7 + [hbm] * 2 + [vmem] * 2,
        out_specs=(vmem,) * 4 + (hbm,) * 4,
        scratch_shapes=list(scratch.values()),
        compiler_params=pltpu.CompilerParams(
            collective_id=0, has_side_effects=True, vmem_limit_bytes=58 * 1024 * 1024
        ),
        name="layers",
    )(
        tokens, cotangent, norm_gains, w_qkv.swapaxes(2, 3), w_attn_out, bias_table.swapaxes(1, 2),
        router.swapaxes(1, 2), w_in[0], w_out[0], routes.swapaxes(1, 2), segments,
    )

    cut = pl.BlockSpec((2, None, ER, 256), lambda e, i: (0, e, 0, i))
    full = pl.BlockSpec((2, None, ER, D), lambda e, i: (0, e, 0, 0))
    out = pl.BlockSpec((1, 256, D), lambda e, i: (e, i, 0))

    def lanes(*lead):
        return pl.BlockSpec(lead + (128,), lambda e, i: (0,) * len(lead) + (3 * e + i,))

    inner, outer, act, grads, qkv_grad, attn_grad, gain_grad, router_grad, bias_grad = pl.pallas_call(
        last_outputs,
        grid=(2, 3),
        out_shape=(
            shape((2, D, D), f32),
            shape((2, D, D), f32),
            shape((ROWS, D), bf16),
            shape((ROWS, D), f32),
            shape((3, HF, D), f32),
            shape((HF, D), f32),
            shape((2, D), f32),
            shape((32, D), f32),
            shape((HEADS, 1, 16), f32),
        ),
        in_specs=[
            cut, full, cut, full, lanes(ROWS), lanes(ROWS), lanes(D), lanes(SMALL),
        ],
        out_specs=(
            out, out, lanes(ROWS), lanes(ROWS), lanes(3, HF), lanes(HF), lanes(2), lanes(32),
            pl.BlockSpec((HEADS, 1, 16), lambda e, i: (0, 0, 0)),
        ),
        compiler_params=pltpu.CompilerParams(vmem_limit_bytes=58 * 1024 * 1024),
        name="last_outputs",
    )(xe.reshape(2, 2, ER, D), dpre, u, de.reshape(2, 2, ER, D), act, grads, dense, small)

    return (
        act[None],
        grads[None],
        gain_grad[None],
        qkv_grad.swapaxes(1, 2)[None],
        attn_grad[None],
        bias_grad.transpose(1, 2, 0),
        router_grad.T[None],
        inner[None],
        outer[None],
    )


def solution(mesh):
    in_specs = (
        P("dp", None),
        P("dp", None),
        P("section", None, None),
        P("section", None, None, "tensor"),
        P("section", "tensor", None),
        P("section", None, "tensor"),
        P("section", None, None),
        P("section", "dp", None, "tensor"),
        P("section", "dp", "tensor", None),
        P("section", "dp", None),
        P("dp", None),
    )
    out_specs = (
        P("section", "dp", None),
        P("section", "dp", None),
        P("section", None, None),
        P("section", None, None, "tensor"),
        P("section", "tensor", None),
        P("section", None, "tensor"),
        P("section", None, None),
        P("section", "dp", None, "tensor"),
        P("section", "dp", "tensor", None),
    )
    return jax.shard_map(body, mesh=mesh, in_specs=in_specs, out_specs=out_specs, check_vma=False)
```

time: 244 us -> 191 us (0.78)
  Pallas kernels: 215 us -> 190 us
  local copies, waits for them, and re-layouts: 15 us -> 0 us
  matrix products: 9.05 us -> 0 us
  other arithmetic: 4.18 us -> 0 us
    pallas_call x1, Pallas kernels: 215 us -> 179 us  [body(): pl.pallas_call(kernel, out_shape=(shape((ROWS, D), bf16), shape((ROWS, D)...]
    unnamed x19 -> x0, local copies, waits for them, and re-layouts: 11.8 us -> none
    pallas_call x0 -> x1, Pallas kernels: none -> 10.6 us  [body(): pl.pallas_call(last_outputs, grid=(2, 3), out_shape=(shape((2, D, D), f32...]
    dot_general x2 -> x0, matrix products: 9.05 us -> none  [the longest x1 5.4 us: body(): inner = jnp.einsum('erd,erf->edf', xe, dpre, preferred_element_type=f32)]
    broadcast_in_dim x3 -> x0, other arithmetic: 3.06 us -> none  [the longest x1 1.52 us: body(): qkv_grad[None]]
where the time goes in v2:
time: 191 us
  Pallas kernels  190 us (99%)
    pallas_call x1, Pallas kernels, body(): pl.pallas_call(kernel, out_shape=(shape((ROWS, D), bf16), shape((ROWS, D)...  179 us
    pallas_call x1, Pallas kernels, body(): pl.pallas_call(last_outputs, grid=(2, 3), out_shape=(shape((2, D, D), f32...  10.6 us

profile of v2, /device:TPU:0, one launch (start us, length us, event | category | flops | bytes accessed | tf_op | source)
XLA Modules:
  0.0 190.7 jit_solution(3890401570054546115)
XLA Ops:
  0.6 179.2 %layers.1 = (bf16[256,768]{1,0:T(8,128)(2,1)}, bf16[256,768]{1,0:T(8,128)(2,1)}, bf16[768,768]{1,0:T(8,128)(2,1)}, f32[48,768]{1,0:T(8,128)}, bf16[2,2,16,16,768...) custom-call(bf16[256,768]{1,0:T(8,128)(2,1)} %tokens.1, ...), custom_call_target="tpu_custom_call" | custom-call | tf_op jit(solution)/shard_map/layers/pallas_call | solution.py:759
  179.9 10.6 %last_outputs.1 = (f32[2,768,768]{2,1,0:T(8,128)}, f32[2,768,768]{2,1,0:T(8,128)}, bf16[256,768]{1,0:T(8,128)(2,1)}, f32[256,768]{1,0:T(8,128)}, f32[3,192,768]{...) custom-call(bf16[2,2,256,768]{3,2,1,0:T(8,128)(2,1)} %bitcast.23, ...), custom_call_target="tpu_custom_call" | custom-call | tf_op jit(solution)/shard_map/last_outputs/pallas_call | solution.py:787

commit v3 on v2

--- a/solution.py
+++ b/solution.py
@@ -53,14 +53,14 @@
 
 
 def kernel(
-    tokens, cotangent, gains, w_qkv, w_att, bias_tab, router, w_in_hbm, w_out_hbm, routes, segments,
-    act_out, grad_out, dense_out, small_out, xe_out, u_out, dpre_out, de_out,
-    xin, gin, w_in, w_out, wall, call, normed, qkv, probs, hidden, hid_scale, normed2, rpad,
+    tokens, cotangent, gains, w_qkv_hbm, w_att, bias_tab, router, w_in_hbm, w_out_hbm, routes, segments,
+    act_out, grad_out, dense_out, small_out, xe_out, act, dpre, de_out,
+    xin, gin, w_qkv, w_in, w_out, wall, part_o, rs_o, o_full, call, normed, qkv, probs, hidden, hid_scale, normed2, rpad,
     gate, slots, hits, ptg, pick, pick_g, send_b, recv_b, send_e, recv_e, send_d, recv_d, send_x,
-    recv_x, act, dact, dpre, part_y, rs_y, part_h, rs_h, dh_own, dh_full, part_a, rs_a, in_full,
+    recv_x, dact, part_y, rs_y, part_h, rs_h, dh_own, dh_full, part_a, rs_a, in_full,
     dq_all, score_sum, gact, dense_s, dense_r, dense_f, small_acc, small_s, small_r, small_z, small_f,
-    ld_sem, out_sem, w_ss, w_rs, c_ss, c_rs, b_ss, b_rs, e_ss, e_rs, d_ss, d_rs, x_ss, x_rs,
-    ry_ss, ry_rs, ay_ss, ay_rs, rh_ss, rh_rs, ah_ss, ah_rs, ra_ss, ra_rs, aa_ss, aa_rs,
+    ld_sem, out_sem, end_sem, w_ss, w_rs, c_ss, c_rs, b_ss, b_rs, e_ss, e_rs, d_ss, d_rs, x_ss, x_rs,
+    ro_ss, ro_rs, ao_ss, ao_rs, ry_ss, ry_rs, ay_ss, ay_rs, rh_ss, rh_rs, ah_ss, ah_rs, ra_ss, ra_rs, aa_ss, aa_rs,
     hand_ss, hand_rs, back_ss, back_rs, dn_ss, dn_rs, df_ss, df_rs, sm_ss, sm_rs, sz_ss, sz_rs,
     sf_ss, sf_rs, turn_sem,
 ):
@@ -72,8 +72,21 @@
 
     load_in = pltpu.make_async_copy(w_in_hbm, w_in, ld_sem.at[0])
     load_out = pltpu.make_async_copy(w_out_hbm, w_out, ld_sem.at[1])
-    load_in.start()
-    load_out.start()
+    load_qkv = pltpu.make_async_copy(w_qkv_hbm, w_qkv, ld_sem.at[2])
+    load_att = pltpu.make_async_copy(w_att, wall.at[mz], ld_sem.at[3])
+    load_x = pltpu.make_async_copy(tokens, xin, ld_sem.at[4])
+    load_g = pltpu.make_async_copy(cotangent, gin, ld_sem.at[4])
+
+    @pl.when(first)
+    def _():
+        load_x.start()
+
+    @pl.when(second)
+    def _():
+        load_g.start()
+
+    load_qkv.start()
+    load_att.start()
 
     barrier = pltpu.get_barrier_semaphore()
 
@@ -175,6 +188,7 @@
         return sems[0].at[b], sems[1].at[b]
 
     c_sem, b_sem, d_sem = (c_ss, c_rs), (b_ss, b_rs), (d_ss, d_rs)
+    ro, ao = (ro_ss, ro_rs), (ao_ss, ao_rs)
     ry, ay, rh = (ry_ss, ry_rs), (ay_ss, ay_rs), (rh_ss, rh_rs)
     ah, ra, aa = (ah_ss, ah_rs), (ra_ss, ra_rs), (aa_ss, aa_rs)
     dn, df = (dn_ss, dn_rs), (df_ss, df_rs)
@@ -217,27 +231,29 @@
         row1 = to_row(slot1.astype(f32)).astype(jnp.int32)
         pick[b] = ((slot_sub == row0) | (slot_sub == row1)).astype(f32).astype(bf16)
 
-    @pl.when(first)
-    def _():
-        xin[...] = tokens[...].reshape(2, TZ, OWN, D)
-
-    @pl.when(second)
-    def _():
-        gin[...] = cotangent[...].reshape(2, TZ, OWN, D)
-
-    wall[mz] = w_att[0]
     gain0 = gains[0, 0:1, :].astype(f32)
     gain1 = gains[0, 1:2, :].astype(f32)
     gap = row - col
     head_of = iota((BLOCK, HF), 1) // (HF // HEADS)
 
-    pl.semaphore_wait(barrier, DP + TZ - 1)
+    @pl.when(first)
+    def _():
+        load_x.wait()
 
     @pl.when(second)
     def _():
+        load_g.wait()
+
+    load_qkv.wait()
+    load_att.wait()
+    load_in.start()
+    load_out.start()
+
+    @pl.when(second)
+    def _():
+        pl.semaphore_wait(barrier, DP + TZ - 1)
         pl.semaphore_wait(turn_sem, 1)
-
-    gather_start(wall, w_ss, w_rs)
+        gather_start(wall, w_ss, w_rs)
 
     for b in range(2):
         rows = slice(b * BLOCK, (b + 1) * BLOCK)
@@ -250,7 +266,7 @@
         x = xin[b].reshape(BLOCK, D).astype(f32)
         normed[rows, :] = (x * rms_scale(x) * gain0).astype(bf16)
         for j in range(3):
-            qkv[j, rows, :] = nt(normed[rows, :], w_qkv[0, j]).astype(bf16)
+            qkv[j, rows, :] = nt(normed[rows, :], w_qkv[j]).astype(bf16)
         seg_row = segments[b : b + 1, :].astype(f32)
         allowed = (gap >= 0) & (seg_row == to_col(seg_row))
         q = qkv[0, rows, :]
@@ -270,7 +286,17 @@
             probs[b * HEADS + h] = prob
             context = jnp.where(head_of == h, nn(prob.astype(bf16), v), context)
         call[b, mz] = context.astype(bf16)
-        gather_start(call.at[b], *both(c_sem, b))
+
+        @pl.when(first)
+        def _():
+            if b == 0:
+                pl.semaphore_wait(barrier, DP + TZ - 1)
+            part_o[b] = nn(call[b, mz], wall[mz]).astype(bf16).reshape(TZ, OWN, D)
+            scatter_start(part_o.at[b], rs_o.at[b], *both(ro, b))
+
+        @pl.when(second)
+        def _():
+            gather_start(call.at[b], *both(c_sem, b))
 
     def dispatch(chosen, values, snd, rcv, sems, b):
         for e in range(2):
@@ -281,23 +307,35 @@
     def dispatch_grad(b):
         dispatch(pick_g, gin[b].reshape(BLOCK, D), send_d, recv_d, d_sem, b)
 
-    for b in range(2):
-        for i in range(1, TZ):
-            gather_recv(call.at[b], *both(c_sem, b), i)
-        if b == 0:
+    @pl.when(first)
+    def _():
+        for b in range(2):
+            o_full[b, mz] = scatter_sum(part_o.at[b], rs_o.at[b], *both(ro, b)).astype(bf16)
+            gather_start(o_full.at[b], *both(ao, b))
+
+    for b in range(2):
+        @pl.when(first)
+        def _():
             for i in range(1, TZ):
-                gather_recv(wall, w_ss, w_rs, i)
-
-            @pl.when(first)
-            def _():
+                gather_recv(o_full.at[b], *both(ao, b), i)
+            if b == 1:
                 pl.semaphore_signal(
                     turn_sem, inc=1, device_id={"section": 1 - sec}, device_id_type=MESH
                 )
-
-        h = xin[b].reshape(BLOCK, D).astype(f32)
-        for t in range(TZ):
-            h += nn(call[b, t], wall[t])
-        hidden[b] = h
+            hidden[b] = xin[b].reshape(BLOCK, D).astype(f32) + o_full[b].reshape(BLOCK, D).astype(f32)
+
+        @pl.when(second)
+        def _():
+            for i in range(1, TZ):
+                gather_recv(call.at[b], *both(c_sem, b), i)
+                if b == 0:
+                    gather_recv(wall, w_ss, w_rs, i)
+            total = xin[b].reshape(BLOCK, D).astype(f32)
+            for t in range(TZ):
+                total += nn(call[b, t], wall[t])
+            hidden[b] = total
+
+        h = hidden[b]
         scale = rms_scale(h)
         hid_scale[b] = scale
         normed2[b] = (h * scale * gain1).astype(bf16)
@@ -420,7 +458,6 @@
 
     for b in range(2):
         save(b, 0, recv_b, xe_out)
-        save(b, 1, act, u_out)
 
     @pl.when(first)
     def _():
@@ -440,14 +477,20 @@
         each_part(expert_backward)
 
     for b in range(2):
-        save(b, 2, recv_d, de_out)
-        save(b, 3, dpre, dpre_out)
+        save(b, 1, recv_d, de_out)
 
     for b in range(2):
         pt0 = (slot_lane == slots[b, :, 0:1]).astype(f32).astype(bf16)
         pt1 = (slot_lane == slots[b, :, 1:2]).astype(f32).astype(bf16)
         for e in range(2):
             swap_recv(send_x.at[b, e], recv_x.at[b, e], x_ss.at[b, e], x_rs.at[b, e])
+        if b == 1:
+            @pl.when(first)
+            def _():
+                pl.semaphore_signal(
+                    turn_sem, inc=1, device_id={"section": 1 - sec}, device_id_type=MESH
+                )
+
         back = recv_x[b].reshape(SLOTS, WIDE)
         q0 = jnp.sum(nn(pt0, back[:, D:]), axis=1, keepdims=True)
         q1 = jnp.sum(nn(pt1, back[:, D:]), axis=1, keepdims=True)
@@ -480,7 +523,7 @@
         rows = slice(b * BLOCK, (b + 1) * BLOCK)
         for i in range(1, TZ):
             gather_recv(dh_full.at[b], *both(ah, b), i)
-        dc = nt(dh_full[b].reshape(BLOCK, D), w_att[0]).astype(bf16)
+        dc = nt(dh_full[b].reshape(BLOCK, D), wall[mz]).astype(bf16)
         q = qkv[0, rows, :]
         k = qkv[1, rows, :]
         v = qkv[2, rows, :]
@@ -502,9 +545,9 @@
         dq_all[0, rows, :] = (dq * 0.125).astype(bf16)
         dq_all[1, rows, :] = (dk * 0.125).astype(bf16)
         dq_all[2, rows, :] = dv.astype(bf16)
-        da = nn(dq_all[0, rows, :], w_qkv[0, 0])
-        da += nn(dq_all[1, rows, :], w_qkv[0, 1])
-        da += nn(dq_all[2, rows, :], w_qkv[0, 2])
+        da = nn(dq_all[0, rows, :], w_qkv[0])
+        da += nn(dq_all[1, rows, :], w_qkv[1])
+        da += nn(dq_all[2, rows, :], w_qkv[2])
         part_a[b] = da.astype(bf16).reshape(TZ, OWN, D)
         scatter_start(part_a.at[b], rs_a.at[b], *both(ra, b))
 
@@ -545,9 +588,7 @@
             def _():
                 dp_copy(small_s.at[j], small_r.at[me], sm_ss, sm_rs, j, me).start()
 
-    @pl.when(first)
-    def _():
-        dense_part()
+    dense_part()
 
     for b in range(2):
         x_own = xin[b, mz].astype(f32)
@@ -570,11 +611,11 @@
             def _():
                 hand(b, lax.rem(mz + i, TZ), back_ss, back_rs, in_full, gin).start()
 
-    grad_out[...] = in_full[...].reshape(ROWS, D)
+    save_grad = pltpu.make_async_copy(in_full, grad_out, end_sem.at[1])
+    save_grad.start()
 
     @pl.when(second)
     def _():
-        dense_part()
         for b in range(2):
             combine(b)
         for b in range(2):
@@ -583,9 +624,14 @@
             for i in range(1, TZ):
                 gather_recv(gact.at[b], *both(ay, b), i)
 
-    act_out[...] = gact[...].reshape(ROWS, D)
+    save_act = pltpu.make_async_copy(gact, act_out, end_sem.at[0])
+    save_act.start()
 
     holds = me < PARTS
+
+    @pl.when(second)
+    def _():
+        pl.semaphore_wait(turn_sem, 1)
 
     for n in range(2):
         swap_recv(dense_s.at[n], dense_r.at[n], *both(dn, n))
@@ -614,9 +660,11 @@
         small_f[me] = total.astype(bf16)
         spread(small_f, sf_ss, sf_rs)
 
-    gather_sent(wall, w_ss, w_rs)
-    for b in range(2):
-        gather_sent(call.at[b], *both(c_sem, b))
+    @pl.when(second)
+    def _():
+        gather_sent(wall, w_ss, w_rs)
+
+    for b in range(2):
         for e in range(2):
             swap_sent(send_b.at[b, e], recv_b.at[b, e], b_ss.at[b, e], b_rs.at[b, e])
             swap_sent(send_e.at[b, e], recv_e.at[b, e], e_ss.at[b, e], e_rs.at[b, e])
@@ -631,11 +679,14 @@
 
         @pl.when(first)
         def _():
+            scatter_sent(part_o.at[b], rs_o.at[b], *both(ro, b))
+            gather_sent(o_full.at[b], *both(ao, b))
             for t in range(TZ):
                 hand(b, t, hand_ss, hand_rs, gact, xin).wait_send()
 
         @pl.when(second)
         def _():
+            gather_sent(call.at[b], *both(c_sem, b))
             for t in range(TZ):
                 hand(b, t, back_ss, back_rs, in_full, gin).wait_send()
 
@@ -655,7 +706,7 @@
         copy.wait()
     for n in range(2):
         spread_recv(dense_f.at[n], *both(df, n))
-        dense_out[:, HALF * n : HALF * (n + 1)] = dense_f[n].reshape(D, HALF)
+        pltpu.make_async_copy(dense_f.at[n], dense_out.at[n], end_sem.at[2 + n]).start()
     for j in range(PARTS):
         @pl.when(me != j)
         def _():
@@ -667,25 +718,46 @@
     small_out[BIAS : BIAS + 1, 0:128] = jnp.sum(jnp.where(mine, held, 0.0), axis=0, keepdims=True)
     for n in range(2):
         spread_sent(dense_f.at[n], *both(df, n))
+    save_act.wait()
+    save_grad.wait()
+    for n in range(2):
+        pltpu.make_async_copy(dense_f.at[n], dense_out.at[n], end_sem.at[2 + n]).wait()
 
 
 def last_outputs(
     xe, dpre, u, de, act, grads, dense, small,
     inner, outer, act_out, grads_out, qkv_out, attn_out, gain_out, router_out, bias_out,
+    inner_v, outer_v, grads_f, dense_f, out_sem,
 ):
-    inner[0] = tn(xe[...].reshape(SLOTS, 256), dpre[...].reshape(SLOTS, D))
-    outer[0] = tn(u[...].reshape(SLOTS, 256), de[...].reshape(SLOTS, D))
-    act_out[...] = act[...]
-    grads_out[...] = grads[...].astype(f32)
-    qkv_out[...] = dense[0 : 3 * HF, :].astype(f32).reshape(3, HF, 128)
-    attn_out[...] = dense[3 * HF :, :].astype(f32)
+    sent = []
+
+    def store(src, dst):
+        copy = pltpu.make_async_copy(src, dst, out_sem.at[len(sent)])
+        copy.start()
+        sent.append(copy)
+
+    store(act, act_out)
+    grads_f[...] = grads[...].reshape(ROWS, D).astype(f32)
+    store(grads_f, grads_out)
+    for n in range(2):
+        dense_f[:, HALF * n : HALF * (n + 1)] = dense[n].reshape(D, HALF).astype(f32)
+    for j in range(3):
+        store(dense_f.at[HF * j : HF * (j + 1)], qkv_out.at[j])
+    store(dense_f.at[3 * HF : D], attn_out)
+    for e in range(2):
+        for one, two, total, out in ((xe, dpre, inner_v, inner), (u, de, outer_v, outer)):
+            right = two[:, e].reshape(SLOTS, D)
+            for i in range(3):
+                cols = slice(256 * i, 256 * (i + 1))
+                left = one[:, e, :, cols] if one is u else one[:, e, :, :, cols]
+                total[e, cols, :] = tn(left.reshape(SLOTS, 256), right)
+                store(total.at[e, cols], out.at[e, cols])
     router_out[...] = small[0:32, :]
     gain_out[...] = small[GAIN0 : GAIN1 + 1, :]
-
-    @pl.when((pl.program_id(0) == 0) & (pl.program_id(1) == 0))
-    def _():
-        for h in range(HEADS):
-            bias_out[h] = small[BIAS : BIAS + 1, 16 * h : 16 * (h + 1)]
+    for h in range(HEADS):
+        bias_out[h] = small[BIAS : BIAS + 1, 16 * h : 16 * (h + 1)]
+    for copy in sent:
+        copy.wait()
 
 
 def body(
@@ -703,9 +775,11 @@
     scratch = dict(
         xin=rows4,
         gin=rows4,
+        w_qkv=pltpu.VMEM((3, HF, D), bf16),
         w_in=pltpu.VMEM((2, D, D), bf16),
         w_out=pltpu.VMEM((2, D, D), bf16),
         wall=pltpu.VMEM((TZ, HF, D), bf16),
+        part_o=rows4, rs_o=rows4, o_full=rows4,
         call=pltpu.VMEM((2, TZ, BLOCK, HF), bf16),
         normed=pltpu.VMEM((ROWS, D), bf16),
         qkv=pltpu.VMEM((3, ROWS, HF), bf16),
@@ -722,7 +796,7 @@
         pick_g=pltpu.VMEM((2, SLOTS, BLOCK), bf16),
         send_b=messages, recv_b=messages, send_e=messages, recv_e=messages,
         send_d=messages, recv_d=messages, send_x=wide, recv_x=wide,
-        act=expert_rows, dact=expert_rows, dpre=expert_rows,
+        dact=expert_rows,
         part_y=rows4, rs_y=rows4, part_h=rows4, rs_h=rows4,
         dh_own=pltpu.VMEM((2, OWN, D), f32),
         dh_full=rows4, part_a=rows4, rs_a=rows4, in_full=rows4,
@@ -734,15 +808,16 @@
         small_s=pieces, small_r=pieces,
         small_z=pltpu.VMEM((TZ, SMALL, 128), bf16),
         small_f=pieces,
-        ld_sem=dma((2,)),
-        out_sem=dma((2, 4)),
+        ld_sem=dma((5,)),
+        out_sem=dma((2, 2)),
+        end_sem=dma((4,)),
         w_ss=dma((TZ,)), w_rs=dma((TZ,)),
         c_ss=dma((2, TZ)), c_rs=dma((2, TZ)),
     )
     for name in ("b", "e", "d", "x"):
         scratch[name + "_ss"] = dma((2, 2, DP))
         scratch[name + "_rs"] = dma((2, 2, DP))
-    for name in ("ry", "ay", "rh", "ah", "ra", "aa", "hand", "back"):
+    for name in ("ro", "ao", "ry", "ay", "rh", "ah", "ra", "aa", "hand", "back"):
         scratch[name + "_ss"] = dma((2, TZ))
         scratch[name + "_rs"] = dma((2, TZ))
     for name in ("dn", "df"):
@@ -754,43 +829,38 @@
     scratch["turn_sem"] = pltpu.SemaphoreType.REGULAR
 
     shape = jax.ShapeDtypeStruct
-    rows = shape((2, 2, DP, PAD, D), bf16)
-    kept = shape((2, 2, ER, D), bf16)
+    near = pltpu.VMEM
     act, grads, dense, small, xe, u, dpre, de = pl.pallas_call(
         kernel,
         out_shape=(
-            shape((ROWS, D), bf16),
-            shape((ROWS, D), bf16),
-            shape((D, D), bf16),
-            shape((SMALL, D), f32),
-            rows, kept, kept, rows,
+            near((2, TZ, OWN, D), bf16),
+            near((2, TZ, OWN, D), bf16),
+            near((2, DP, CUT, HALF), bf16),
+            near((SMALL, D), f32),
+            near((2, 2, DP, PAD, D), bf16),
+            near((2, 2, ER, D), bf16),
+            near((2, 2, ER, D), bf16),
+            near((2, 2, DP, PAD, D), bf16),
         ),
-        in_specs=[vmem] * 7 + [hbm] * 2 + [vmem] * 2,
-        out_specs=(vmem,) * 4 + (hbm,) * 4,
+        in_specs=[hbm, hbm, vmem, hbm, hbm, vmem, vmem, hbm, hbm, vmem, vmem],
+        out_specs=(vmem,) * 8,
         scratch_shapes=list(scratch.values()),
         compiler_params=pltpu.CompilerParams(
-            collective_id=0, has_side_effects=True, vmem_limit_bytes=58 * 1024 * 1024
+            collective_id=0, has_side_effects=True, vmem_limit_bytes=55 * 1024 * 1024
         ),
         name="layers",
     )(
-        tokens, cotangent, norm_gains, w_qkv.swapaxes(2, 3), w_attn_out, bias_table.swapaxes(1, 2),
+        tokens.reshape(2, TZ, OWN, D), cotangent.reshape(2, TZ, OWN, D), norm_gains,
+        w_qkv[0].swapaxes(1, 2), w_attn_out[0], bias_table.swapaxes(1, 2),
         router.swapaxes(1, 2), w_in[0], w_out[0], routes.swapaxes(1, 2), segments,
     )
 
-    cut = pl.BlockSpec((2, None, ER, 256), lambda e, i: (0, e, 0, i))
-    full = pl.BlockSpec((2, None, ER, D), lambda e, i: (0, e, 0, 0))
-    out = pl.BlockSpec((1, 256, D), lambda e, i: (e, i, 0))
-
-    def lanes(*lead):
-        return pl.BlockSpec(lead + (128,), lambda e, i: (0,) * len(lead) + (3 * e + i,))
-
     inner, outer, act, grads, qkv_grad, attn_grad, gain_grad, router_grad, bias_grad = pl.pallas_call(
         last_outputs,
-        grid=(2, 3),
         out_shape=(
             shape((2, D, D), f32),
             shape((2, D, D), f32),
-            shape((ROWS, D), bf16),
+            shape((2, TZ, OWN, D), bf16),
             shape((ROWS, D), f32),
             shape((3, HF, D), f32),
             shape((HF, D), f32),
@@ -798,19 +868,21 @@
             shape((32, D), f32),
             shape((HEADS, 1, 16), f32),
         ),
-        in_specs=[
-            cut, full, cut, full, lanes(ROWS), lanes(ROWS), lanes(D), lanes(SMALL),
+        in_specs=[vmem] * 8,
+        out_specs=(hbm,) * 6 + (vmem,) * 3,
+        scratch_shapes=[
+            pltpu.VMEM((2, D, D), f32),
+            pltpu.VMEM((2, D, D), f32),
+            pltpu.VMEM((ROWS, D), f32),
+            pltpu.VMEM((D, D), f32),
+            dma((18,)),
         ],
-        out_specs=(
-            out, out, lanes(ROWS), lanes(ROWS), lanes(3, HF), lanes(HF), lanes(2), lanes(32),
-            pl.BlockSpec((HEADS, 1, 16), lambda e, i: (0, 0, 0)),
-        ),
-        compiler_params=pltpu.CompilerParams(vmem_limit_bytes=58 * 1024 * 1024),
+        compiler_params=pltpu.CompilerParams(vmem_limit_bytes=20 * 1024 * 1024),
         name="last_outputs",
-    )(xe.reshape(2, 2, ER, D), dpre, u, de.reshape(2, 2, ER, D), act, grads, dense, small)
+    )(xe, dpre, u, de, act, grads, dense, small)
 
     return (
-        act[None],
+        act.reshape(ROWS, D)[None],
         grads[None],
         gain_grad[None],
         qkv_grad.swapaxes(1, 2)[None],

time: 191 us -> 169 us (0.88)
  Pallas kernels: 190 us -> 168 us
    pallas_call x2, Pallas kernels: 190 us -> 168 us  [the longest x1 163 us: body(): pl.pallas_call(kernel, out_shape=(near((2, TZ, OWN, D), bf16), near((2, T...]
where the time goes in v3:
time: 169 us
  Pallas kernels  168 us (99%)
    pallas_call x1, Pallas kernels, body(): pl.pallas_call(kernel, out_shape=(near((2, TZ, OWN, D), bf16), near((2, T...  163 us
    pallas_call x1, Pallas kernels, body(): pl.pallas_call(last_outputs, out_shape=(shape((2, D, D), f32), shape((2,...  5.79 us

profile of v3, /device:TPU:0, one launch (start us, length us, event | category | flops | bytes accessed | tf_op | source)
XLA Modules:
  0.0 169.3 jit_solution(1981428027984470356)
XLA Ops:
  0.6 162.7 %layers.1 = (bf16[2,4,32,768]{3,2,1,0:T(8,128)(2,1)S(1)}, bf16[2,4,32,768]{3,2,1,0:T(8,128)(2,1)S(1)}, bf16[2,16,48,384]{3,2,1,0:T(8,128)(2,1)S(1)}, f32[48,768]...) custom-call(bf16[2,4,32,768]{3,2,1,0:T(8,128)(2,1)} %bitcast.27, ...), custom_call_target="tpu_custom_call" | custom-call | tf_op jit(solution)/shard_map/layers/pallas_call | solution.py:833
  163.3 5.8 %last_outputs.1 = (f32[2,768,768]{2,1,0:T(8,128)}, f32[2,768,768]{2,1,0:T(8,128)}, bf16[2,4,32,768]{3,2,1,0:T(8,128)(2,1)}, f32[256,768]{1,0:T(8,128)}, f32[3,19...) custom-call(bf16[2,2,16,16,768]{4,3,2,1,0:T(8,128)(2,1)S(1)} %get-tuple-, ...), custom_call_target="tpu_custom_call" | custom-call | tf_op jit(solution)/shard_map/last_outputs/pallas_call | solution.py:858

commit v4 on v3

--- a/solution.py
+++ b/solution.py
@@ -103,47 +103,50 @@
         )
     pl.semaphore_signal(barrier, inc=1, device_id={"section": 1 - sec}, device_id_type=MESH)
 
-    def z_copy(src, dst, ss, rs, peer, slot):
+    def z_copy(src, dst, ss, rs, peer):
         return pltpu.make_async_remote_copy(
-            src_ref=src, dst_ref=dst, send_sem=ss.at[peer], recv_sem=rs.at[slot],
+            src_ref=src, dst_ref=dst, send_sem=ss, recv_sem=rs,
             device_id={"tensor": peer}, device_id_type=MESH,
         )
 
+    def z_round(buf, ss, rs):
+        part = buf.at[pl.ds(0, TZ - 1)]
+        return z_copy(part, part, ss, rs, lax.rem(mz + 1, TZ))
+
     def gather_start(buf, ss, rs):
         for i in range(1, TZ):
-            z_copy(buf.at[mz], buf.at[mz], ss, rs, lax.rem(mz + i, TZ), mz).start()
-
-    def gather_recv(buf, ss, rs, i):
-        src = lax.rem(mz + i, TZ)
-        z_copy(buf.at[src], buf.at[src], ss, rs, src, src).wait_recv()
+            z_copy(buf.at[mz], buf.at[mz], ss, rs, lax.rem(mz + i, TZ)).start()
+
+    def gather_recv(buf, ss, rs):
+        z_round(buf, ss, rs).wait_recv()
 
     def gather_sent(buf, ss, rs):
-        for i in range(1, TZ):
-            z_copy(buf.at[mz], buf.at[mz], ss, rs, lax.rem(mz + i, TZ), mz).wait_send()
+        z_round(buf, ss, rs).wait_send()
 
     def scatter_start(part, rcv, ss, rs):
         for i in range(1, TZ):
             peer = lax.rem(mz + i, TZ)
-            z_copy(part.at[peer], rcv.at[mz], ss, rs, peer, mz).start()
+            z_copy(part.at[peer], rcv.at[mz], ss, rs, peer).start()
 
     def scatter_sum(part, rcv, ss, rs):
+        z_round(rcv, ss, rs).wait_recv()
         total = part[mz].astype(f32)
         for i in range(1, TZ):
-            src = lax.rem(mz + i, TZ)
-            z_copy(part.at[src], rcv.at[src], ss, rs, src, src).wait_recv()
-            total += rcv[src].astype(f32)
+            total += rcv[lax.rem(mz + i, TZ)].astype(f32)
         return total
 
     def scatter_sent(part, rcv, ss, rs):
-        for i in range(1, TZ):
-            peer = lax.rem(mz + i, TZ)
-            z_copy(part.at[peer], rcv.at[mz], ss, rs, peer, mz).wait_send()
-
-    def dp_copy(src, dst, ss, rs, peer, slot):
+        z_round(part, ss, rs).wait_send()
+
+    def dp_copy(src, dst, ss, rs, peer):
         return pltpu.make_async_remote_copy(
-            src_ref=src, dst_ref=dst, send_sem=ss.at[peer], recv_sem=rs.at[slot],
+            src_ref=src, dst_ref=dst, send_sem=ss, recv_sem=rs,
             device_id={"dp": peer}, device_id_type=MESH,
         )
+
+    def dp_round(buf, ss, rs, count=DP - 1):
+        part = buf.at[pl.ds(0, count)]
+        return dp_copy(part, part, ss, rs, lax.rem(me + 1, DP))
 
     def others(step):
         def one(i, carry):
@@ -152,36 +155,35 @@
 
         lax.fori_loop(1, DP, one, 0)
 
-    def others_back(step):
-        def one(i, carry):
-            step(lax.rem(me + DP - i, DP))
-            return carry
-
-        lax.fori_loop(1, DP, one, 0)
-
     def swap_start(snd, rcv, ss, rs):
-        others(lambda peer: dp_copy(snd.at[peer], rcv.at[me], ss, rs, peer, me).start())
+        others(lambda peer: dp_copy(snd.at[peer], rcv.at[me], ss, rs, peer).start())
         rcv[me] = snd[me]
 
     def swap_recv(snd, rcv, ss, rs):
-        others_back(lambda src: dp_copy(snd.at[src], rcv.at[src], ss, rs, src, src).wait_recv())
+        dp_round(rcv, ss, rs).wait_recv()
 
     def swap_sent(snd, rcv, ss, rs):
-        others(lambda peer: dp_copy(snd.at[peer], rcv.at[me], ss, rs, peer, me).wait_send())
+        dp_round(snd, ss, rs).wait_send()
 
     def spread(buf, ss, rs):
-        others(lambda peer: dp_copy(buf.at[me], buf.at[me], ss, rs, peer, me).start())
+        others(lambda peer: dp_copy(buf.at[me], buf.at[me], ss, rs, peer).start())
 
     def spread_recv(buf, ss, rs):
-        others_back(lambda src: dp_copy(buf.at[src], buf.at[src], ss, rs, src, src).wait_recv())
+        dp_round(buf, ss, rs).wait_recv()
 
     def spread_sent(buf, ss, rs):
-        others(lambda peer: dp_copy(buf.at[me], buf.at[me], ss, rs, peer, me).wait_send())
+        dp_round(buf, ss, rs).wait_send()
 
     def hand(b, t, ss, rs, src, dst):
         return pltpu.make_async_remote_copy(
-            src_ref=src.at[b, t], dst_ref=dst.at[b, t], send_sem=ss.at[b, t],
-            recv_sem=rs.at[b, t], device_id={"section": 1 - sec}, device_id_type=MESH,
+            src_ref=src.at[b, t], dst_ref=dst.at[b, t], send_sem=ss.at[b],
+            recv_sem=rs.at[b], device_id={"section": 1 - sec}, device_id_type=MESH,
+        )
+
+    def hand_all(b, ss, rs, src, dst):
+        return pltpu.make_async_remote_copy(
+            src_ref=src.at[b], dst_ref=dst.at[b], send_sem=ss.at[b],
+            recv_sem=rs.at[b], device_id={"section": 1 - sec}, device_id_type=MESH,
         )
 
     def both(sems, b):
@@ -253,15 +255,14 @@
     def _():
         pl.semaphore_wait(barrier, DP + TZ - 1)
         pl.semaphore_wait(turn_sem, 1)
-        gather_start(wall, w_ss, w_rs)
+        gather_start(wall, w_ss.at[0], w_rs.at[0])
 
     for b in range(2):
         rows = slice(b * BLOCK, (b + 1) * BLOCK)
 
         @pl.when(second)
         def _():
-            for t in range(TZ):
-                hand(b, t, hand_ss, hand_rs, gact, xin).wait_recv()
+            hand_all(b, hand_ss, hand_rs, gact, xin).wait_recv()
 
         x = xin[b].reshape(BLOCK, D).astype(f32)
         normed[rows, :] = (x * rms_scale(x) * gain0).astype(bf16)
@@ -316,8 +317,7 @@
     for b in range(2):
         @pl.when(first)
         def _():
-            for i in range(1, TZ):
-                gather_recv(o_full.at[b], *both(ao, b), i)
+            gather_recv(o_full.at[b], *both(ao, b))
             if b == 1:
                 pl.semaphore_signal(
                     turn_sem, inc=1, device_id={"section": 1 - sec}, device_id_type=MESH
@@ -326,10 +326,9 @@
 
         @pl.when(second)
         def _():
-            for i in range(1, TZ):
-                gather_recv(call.at[b], *both(c_sem, b), i)
-                if b == 0:
-                    gather_recv(wall, w_ss, w_rs, i)
+            gather_recv(call.at[b], *both(c_sem, b))
+            if b == 0:
+                gather_recv(wall, w_ss.at[0], w_rs.at[0])
             total = xin[b].reshape(BLOCK, D).astype(f32)
             for t in range(TZ):
                 total += nn(call[b, t], wall[t])
@@ -467,12 +466,11 @@
             settle(b)
             hand(b, mz, hand_ss, hand_rs, gact, xin).start()
         for b in range(2):
+            gather_recv(gact.at[b], *both(ay, b))
             for i in range(1, TZ):
-                gather_recv(gact.at[b], *both(ay, b), i)
                 hand(b, lax.rem(mz + i, TZ), hand_ss, hand_rs, gact, xin).start()
         for b in range(2):
-            for t in range(TZ):
-                hand(b, t, back_ss, back_rs, in_full, gin).wait_recv()
+            hand_all(b, back_ss, back_rs, in_full, gin).wait_recv()
             dispatch_grad(b)
         each_part(expert_backward)
 
@@ -521,8 +519,7 @@
 
     for b in range(2):
         rows = slice(b * BLOCK, (b + 1) * BLOCK)
-        for i in range(1, TZ):
-            gather_recv(dh_full.at[b], *both(ah, b), i)
+        gather_recv(dh_full.at[b], *both(ah, b))
         dc = nt(dh_full[b].reshape(BLOCK, D), wall[mz]).astype(bf16)
         q = qkv[0, rows, :]
         k = qkv[1, rows, :]
@@ -586,7 +583,7 @@
 
             @pl.when(me != j)
             def _():
-                dp_copy(small_s.at[j], small_r.at[me], sm_ss, sm_rs, j, me).start()
+                dp_copy(small_s.at[j], small_r.at[me], sm_ss.at[0], sm_rs.at[0], j).start()
 
     dense_part()
 
@@ -604,11 +601,11 @@
             hand(b, mz, back_ss, back_rs, in_full, gin).start()
 
     for b in range(2):
-        for i in range(1, TZ):
-            gather_recv(in_full.at[b], *both(aa, b), i)
-
-            @pl.when(second)
-            def _():
+        gather_recv(in_full.at[b], *both(aa, b))
+
+        @pl.when(second)
+        def _():
+            for i in range(1, TZ):
                 hand(b, lax.rem(mz + i, TZ), back_ss, back_rs, in_full, gin).start()
 
     save_grad = pltpu.make_async_copy(in_full, grad_out, end_sem.at[1])
@@ -621,8 +618,7 @@
         for b in range(2):
             settle(b)
         for b in range(2):
-            for i in range(1, TZ):
-                gather_recv(gact.at[b], *both(ay, b), i)
+            gather_recv(gact.at[b], *both(ay, b))
 
     save_act = pltpu.make_async_copy(gact, act_out, end_sem.at[0])
     save_act.start()
@@ -644,25 +640,22 @@
     @pl.when(holds)
     def _():
         small_r[me] = small_s[me]
-        others_back(
-            lambda src: dp_copy(small_s.at[src], small_r.at[src], sm_ss, sm_rs, src, src).wait_recv()
-        )
+        dp_round(small_r, sm_ss.at[0], sm_rs.at[0]).wait_recv()
         total = small_r[0].astype(f32)
         for p in range(1, DP):
             total += small_r[p].astype(f32)
         small_z[mz] = total.astype(bf16)
-        gather_start(small_z, sz_ss, sz_rs)
-        for i in range(1, TZ):
-            gather_recv(small_z, sz_ss, sz_rs, i)
+        gather_start(small_z, sz_ss.at[0], sz_rs.at[0])
+        gather_recv(small_z, sz_ss.at[0], sz_rs.at[0])
         total = small_z[0].astype(f32)
         for t in range(1, TZ):
             total += small_z[t].astype(f32)
         small_f[me] = total.astype(bf16)
-        spread(small_f, sf_ss, sf_rs)
+        spread(small_f, sf_ss.at[0], sf_rs.at[0])
 
     @pl.when(second)
     def _():
-        gather_sent(wall, w_ss, w_rs)
+        gather_sent(wall, w_ss.at[0], w_rs.at[0])
 
     for b in range(2):
         for e in range(2):
@@ -681,37 +674,41 @@
         def _():
             scatter_sent(part_o.at[b], rs_o.at[b], *both(ro, b))
             gather_sent(o_full.at[b], *both(ao, b))
-            for t in range(TZ):
-                hand(b, t, hand_ss, hand_rs, gact, xin).wait_send()
+            hand_all(b, hand_ss, hand_rs, gact, xin).wait_send()
 
         @pl.when(second)
         def _():
             gather_sent(call.at[b], *both(c_sem, b))
-            for t in range(TZ):
-                hand(b, t, back_ss, back_rs, in_full, gin).wait_send()
+            hand_all(b, back_ss, back_rs, in_full, gin).wait_send()
 
     for n in range(2):
         swap_sent(dense_s.at[n], dense_r.at[n], *both(dn, n))
-    for j in range(PARTS):
-        @pl.when(me != j)
-        def _():
-            dp_copy(small_s.at[j], small_r.at[me], sm_ss, sm_rs, j, me).wait_send()
 
     @pl.when(holds)
     def _():
-        gather_sent(small_z, sz_ss, sz_rs)
-        spread_sent(small_f, sf_ss, sf_rs)
+        dp_round(small_s, sm_ss.at[0], sm_rs.at[0], PARTS - 1).wait_send()
+        gather_sent(small_z, sz_ss.at[0], sz_rs.at[0])
+        spread_sent(small_f, sf_ss.at[0], sf_rs.at[0])
+
+    @pl.when(jnp.logical_not(holds))
+    def _():
+        dp_round(small_s, sm_ss.at[0], sm_rs.at[0], PARTS).wait_send()
 
     for copy in saved:
         copy.wait()
     for n in range(2):
         spread_recv(dense_f.at[n], *both(df, n))
         pltpu.make_async_copy(dense_f.at[n], dense_out.at[n], end_sem.at[2 + n]).start()
+
+    @pl.when(holds)
+    def _():
+        dp_round(small_f, sf_ss.at[0], sf_rs.at[0], PARTS - 1).wait_recv()
+
+    @pl.when(jnp.logical_not(holds))
+    def _():
+        dp_round(small_f, sf_ss.at[0], sf_rs.at[0], PARTS).wait_recv()
+
     for j in range(PARTS):
-        @pl.when(me != j)
-        def _():
-            dp_copy(small_f.at[j], small_f.at[j], sf_ss, sf_rs, j, j).wait_recv()
-
         small_out[:, 128 * j : 128 * (j + 1)] = small_f[j].astype(f32)
     held = small_f[0].astype(f32)
     mine = iota((SMALL, 128), 0) == BIAS + mz
@@ -811,21 +808,18 @@
         ld_sem=dma((5,)),
         out_sem=dma((2, 2)),
         end_sem=dma((4,)),
-        w_ss=dma((TZ,)), w_rs=dma((TZ,)),
-        c_ss=dma((2, TZ)), c_rs=dma((2, TZ)),
+        w_ss=dma((1,)), w_rs=dma((1,)),
+        c_ss=dma((2,)), c_rs=dma((2,)),
     )
     for name in ("b", "e", "d", "x"):
-        scratch[name + "_ss"] = dma((2, 2, DP))
-        scratch[name + "_rs"] = dma((2, 2, DP))
-    for name in ("ro", "ao", "ry", "ay", "rh", "ah", "ra", "aa", "hand", "back"):
-        scratch[name + "_ss"] = dma((2, TZ))
-        scratch[name + "_rs"] = dma((2, TZ))
-    for name in ("dn", "df"):
-        scratch[name + "_ss"] = dma((2, DP))
-        scratch[name + "_rs"] = dma((2, DP))
-    for name, count in (("sm", DP), ("sz", TZ), ("sf", DP)):
-        scratch[name + "_ss"] = dma((count,))
-        scratch[name + "_rs"] = dma((count,))
+        scratch[name + "_ss"] = dma((2, 2))
+        scratch[name + "_rs"] = dma((2, 2))
+    for name in ("ro", "ao", "ry", "ay", "rh", "ah", "ra", "aa", "hand", "back", "dn", "df"):
+        scratch[name + "_ss"] = dma((2,))
+        scratch[name + "_rs"] = dma((2,))
+    for name in ("sm", "sz", "sf"):
+        scratch[name + "_ss"] = dma((1,))
+        scratch[name + "_rs"] = dma((1,))
     scratch["turn_sem"] = pltpu.SemaphoreType.REGULAR
 
     shape = jax.ShapeDtypeStruct

time: 169 us -> 161 us (0.953)
  Pallas kernels: 168 us -> 160 us
    pallas_call x1, Pallas kernels: 163 us -> 154 us  [body(): pl.pallas_call(kernel, out_shape=(near((2, TZ, OWN, D), bf16), near((2, T...]
where the time goes in v4:
time: 161 us
  Pallas kernels  160 us (99%)
    pallas_call x1, Pallas kernels, body(): pl.pallas_call(kernel, out_shape=(near((2, TZ, OWN, D), bf16), near((2, T...  154 us
    pallas_call x1, Pallas kernels, body(): pl.pallas_call(last_outputs, out_shape=(shape((2, D, D), f32), shape((2,...  5.79 us

profile of v4, /device:TPU:0, one launch (start us, length us, event | category | flops | bytes accessed | tf_op | source)
XLA Modules:
  0.0 160.8 jit_solution(9902055040192007891)
XLA Ops:
  0.6 154.2 %layers.1 = (bf16[2,4,32,768]{3,2,1,0:T(8,128)(2,1)S(1)}, bf16[2,4,32,768]{3,2,1,0:T(8,128)(2,1)S(1)}, bf16[2,16,48,384]{3,2,1,0:T(8,128)(2,1)S(1)}, f32[48,768]...) custom-call(bf16[2,4,32,768]{3,2,1,0:T(8,128)(2,1)} %bitcast.27, ...), custom_call_target="tpu_custom_call" | custom-call | tf_op jit(solution)/shard_map/layers/pallas_call | solution.py:827
  154.9 5.8 %last_outputs.1 = (f32[2,768,768]{2,1,0:T(8,128)}, f32[2,768,768]{2,1,0:T(8,128)}, bf16[2,4,32,768]{3,2,1,0:T(8,128)(2,1)}, f32[256,768]{1,0:T(8,128)}, f32[3,19...) custom-call(bf16[2,2,16,16,768]{4,3,2,1,0:T(8,128)(2,1)S(1)} %get-tuple-, ...), custom_call_target="tpu_custom_call" | custom-call | tf_op jit(solution)/shard_map/last_outputs/pallas_call | solution.py:852

commit v5 on v4

--- a/solution.py
+++ b/solution.py
@@ -23,13 +23,14 @@
 PAD = 16
 ER = DP * PAD
 SLOTS = 2 * ER
-WIDE = D + 128
+GATE_ROW = 12
 CUT = D // DP
 SMALL = 48
 GAIN0, GAIN1, BIAS = 32, 33, 34
 HALF = D // 2
 PARTS = D // 128
 EDGES = (0,) + bucket_edges
+FAR_FIRST = (2, 1, 3)
 
 
 def nn(a, b):
@@ -114,7 +115,7 @@
         return z_copy(part, part, ss, rs, lax.rem(mz + 1, TZ))
 
     def gather_start(buf, ss, rs):
-        for i in range(1, TZ):
+        for i in FAR_FIRST:
             z_copy(buf.at[mz], buf.at[mz], ss, rs, lax.rem(mz + i, TZ)).start()
 
     def gather_recv(buf, ss, rs):
@@ -124,7 +125,7 @@
         z_round(buf, ss, rs).wait_send()
 
     def scatter_start(part, rcv, ss, rs):
-        for i in range(1, TZ):
+        for i in FAR_FIRST:
             peer = lax.rem(mz + i, TZ)
             z_copy(part.at[peer], rcv.at[mz], ss, rs, peer).start()
 
@@ -148,12 +149,17 @@
         part = buf.at[pl.ds(0, count)]
         return dp_copy(part, part, ss, rs, lax.rem(me + 1, DP))
 
+    me_x, me_y = me // 4, me % 4
+
+    def away(i):
+        return 2 + ((i + 1) // 2) * (1 - 2 * (i % 2))
+
     def others(step):
         def one(i, carry):
-            step(lax.rem(me + i, DP))
+            step(((me_x + away(i // 4)) % 4) * 4 + (me_y + away(i % 4)) % 4)
             return carry
 
-        lax.fori_loop(1, DP, one, 0)
+        lax.fori_loop(0, DP - 1, one, 0)
 
     def swap_start(snd, rcv, ss, rs):
         others(lambda peer: dp_copy(snd.at[peer], rcv.at[me], ss, rs, peer).start())
@@ -398,13 +404,18 @@
             grad = nt(de, w_out[e, cols, :])
             dpre[b, e, :, cols] = (grad * dact[b, e, :, cols].astype(f32)).astype(bf16)
         out = nt(dpre[b, e], w_in[e])
-        send_x[b, e, :, :, 0:D] = out.astype(bf16).reshape(DP, PAD, D)
+        send_x[b, e] = out.astype(bf16).reshape(DP, PAD, D)
         rows = send_e[b, e].reshape(ER, D).astype(f32)
         weight = jnp.sum(rows * de.astype(f32), axis=1, keepdims=True)
-        coarse = weight.astype(bf16).astype(f32)
-        place = iota((ER, 128), 1)
-        pair = jnp.where(place == 0, coarse, jnp.where(place == 1, weight - coarse, 0.0))
-        send_x[b, e, :, :, D:] = pair.astype(bf16).reshape(DP, PAD, 128)
+        slot = iota((ER, 128), 0) % PAD
+        spread_out = jnp.where(iota((ER, 128), 1) == slot, weight, 0.0).reshape(DP, PAD, 128)
+        line = jnp.sum(spread_out, axis=1, keepdims=True)
+        coarse = line.astype(bf16).astype(f32)
+        place = iota((DP, PAD, 128), 1)
+        extra = jnp.where(place == GATE_ROW, coarse, 0.0)
+        extra += jnp.where(place == GATE_ROW + 1, line - coarse, 0.0)
+        near = out[:, 0:128].reshape(DP, PAD, 128) + extra
+        send_x[b, e, :, :, 0:128] = near.astype(bf16)
         swap_start(send_x.at[b, e], recv_x.at[b, e], x_ss.at[b, e], x_rs.at[b, e])
 
     def each_expert(step):
@@ -489,12 +500,20 @@
                     turn_sem, inc=1, device_id={"section": 1 - sec}, device_id_type=MESH
                 )
 
-        back = recv_x[b].reshape(SLOTS, WIDE)
-        q0 = jnp.sum(nn(pt0, back[:, D:]), axis=1, keepdims=True)
-        q1 = jnp.sum(nn(pt1, back[:, D:]), axis=1, keepdims=True)
+        back = recv_x[b].reshape(SLOTS, D)
+
+        def gate_product(slot):
+            line = slot - slot % PAD + GATE_ROW
+            both_rows = ((slot_lane == line) | (slot_lane == line + 1)).astype(f32).astype(bf16)
+            found = nn(both_rows, back[:, 0:128])
+            mine = iota((BLOCK, 128), 1) == slot % PAD
+            return jnp.sum(jnp.where(mine, found, 0.0), axis=1, keepdims=True)
+
+        q0 = gate_product(slots[b, :, 0:1])
+        q1 = gate_product(slots[b, :, 1:2])
         dc = gate[b, :, 1:2] * q0 - gate[b, :, 0:1] * q1
         dz = ((hits[b, 0] - hits[b, 1]) * dc).astype(bf16)
-        db = nn(pt0 + pt1, back[:, 0:D]) + nn(dz, rpad[...])
+        db = nn(pt0 + pt1, back) + nn(dz, rpad[...])
         part_h[b] = db.astype(bf16).reshape(TZ, OWN, D)
         scatter_start(part_h.at[b], rs_h.at[b], *both(rh, b))
         unit = (lane == GAIN1).astype(f32).astype(bf16)
@@ -765,7 +784,6 @@
     dma = pltpu.SemaphoreType.DMA
     rows4 = pltpu.VMEM((2, TZ, OWN, D), bf16)
     messages = pltpu.VMEM((2, 2, DP, PAD, D), bf16)
-    wide = pltpu.VMEM((2, 2, DP, PAD, WIDE), bf16)
     expert_rows = pltpu.VMEM((2, 2, ER, D), bf16)
     cuts = pltpu.VMEM((2, DP, CUT, HALF), bf16)
     pieces = pltpu.VMEM((DP, SMALL, 128), bf16)
@@ -792,7 +810,7 @@
         pick=pltpu.VMEM((2, SLOTS, BLOCK), bf16),
         pick_g=pltpu.VMEM((2, SLOTS, BLOCK), bf16),
         send_b=messages, recv_b=messages, send_e=messages, recv_e=messages,
-        send_d=messages, recv_d=messages, send_x=wide, recv_x=wide,
+        send_d=messages, recv_d=messages, send_x=messages, recv_x=messages,
         dact=expert_rows,
         part_y=rows4, rs_y=rows4, part_h=rows4, rs_h=rows4,
         dh_own=pltpu.VMEM((2, OWN, D), f32),

time: 161 us -> 155 us (0.963)
  Pallas kernels: 160 us -> 154 us
    pallas_call x1, Pallas kernels: 154 us -> 149 us  [body(): pl.pallas_call(kernel, out_shape=(near((2, TZ, OWN, D), bf16), near((2, T...]
where the time goes in v5:
time: 155 us
  Pallas kernels  154 us (99%)
    pallas_call x1, Pallas kernels, body(): pl.pallas_call(kernel, out_shape=(near((2, TZ, OWN, D), bf16), near((2, T...  149 us
    pallas_call x1, Pallas kernels, body(): pl.pallas_call(last_outputs, out_shape=(shape((2, D, D), f32), shape((2,...  5.79 us

profile of v5, /device:TPU:0, one launch (start us, length us, event | category | flops | bytes accessed | tf_op | source)
XLA Modules:
  0.0 155.2 jit_solution(15756575884613060768)
XLA Ops:
  0.6 148.6 %layers.1 = (bf16[2,4,32,768]{3,2,1,0:T(8,128)(2,1)S(1)}, bf16[2,4,32,768]{3,2,1,0:T(8,128)(2,1)S(1)}, bf16[2,16,48,384]{3,2,1,0:T(8,128)(2,1)S(1)}, f32[48,768]...) custom-call(bf16[2,4,32,768]{3,2,1,0:T(8,128)(2,1)} %bitcast.27, ...), custom_call_target="tpu_custom_call" | custom-call | tf_op jit(solution)/shard_map/layers/pallas_call | solution.py:845
  149.2 5.8 %last_outputs.1 = (f32[2,768,768]{2,1,0:T(8,128)}, f32[2,768,768]{2,1,0:T(8,128)}, bf16[2,4,32,768]{3,2,1,0:T(8,128)(2,1)}, f32[256,768]{1,0:T(8,128)}, f32[3,19...) custom-call(bf16[2,2,16,16,768]{4,3,2,1,0:T(8,128)(2,1)S(1)} %get-tuple-, ...), custom_call_target="tpu_custom_call" | custom-call | tf_op jit(solution)/shard_map/last_outputs/pallas_call | solution.py:870

commit v6 on v5

--- a/solution.py
+++ b/solution.py
@@ -155,11 +155,21 @@
         return 2 + ((i + 1) // 2) * (1 - 2 * (i % 2))
 
     def others(step):
-        def one(i, carry):
-            step(((me_x + away(i // 4)) % 4) * 4 + (me_y + away(i % 4)) % 4)
+        def one(i, j):
+            step(((me_x + away(i)) % 4) * 4 + (me_y + away(j)) % 4)
+
+        def pair(n, carry):
+            j = 1 + (n + 1) // 2 - n // 5
+            i = n - j * (j - 1) // 2
+            one(i, j)
+            one(j, i)
             return carry
 
-        lax.fori_loop(0, DP - 1, one, 0)
+        one(0, 0)
+        lax.fori_loop(0, 2, pair, 0)
+        one(1, 1)
+        one(2, 2)
+        lax.fori_loop(2, 6, pair, 0)
 
     def swap_start(snd, rcv, ss, rs):
         others(lambda peer: dp_copy(snd.at[peer], rcv.at[me], ss, rs, peer).start())

time: 155 us -> 154 us (level)
  Pallas kernels: 154 us -> 152 us
    pallas_call x1, Pallas kernels: 149 us -> 147 us  [body(): pl.pallas_call(kernel, out_shape=(near((2, TZ, OWN, D), bf16), near((2, T...]
where the time goes in v6:
time: 154 us; the launch traced here: 153 us
  Pallas kernels  152 us (99%)
    pallas_call x1, Pallas kernels, body(): pl.pallas_call(kernel, out_shape=(near((2, TZ, OWN, D), bf16), near((2, T...  147 us
    pallas_call x1, Pallas kernels, body(): pl.pallas_call(last_outputs, out_shape=(shape((2, D, D), f32), shape((2,...  5.79 us

profile of v6, /device:TPU:0, one launch (start us, length us, event | category | flops | bytes accessed | tf_op | source)
XLA Modules:
  0.0 153.2 jit_solution(16723066151576060144)
XLA Ops:
  0.6 146.6 %layers.1 = (bf16[2,4,32,768]{3,2,1,0:T(8,128)(2,1)S(1)}, bf16[2,4,32,768]{3,2,1,0:T(8,128)(2,1)S(1)}, bf16[2,16,48,384]{3,2,1,0:T(8,128)(2,1)S(1)}, f32[48,768]...) custom-call(bf16[2,4,32,768]{3,2,1,0:T(8,128)(2,1)} %bitcast.27, ...), custom_call_target="tpu_custom_call" | custom-call | tf_op jit(solution)/shard_map/layers/pallas_call | solution.py:855
  147.3 5.8 %last_outputs.1 = (f32[2,768,768]{2,1,0:T(8,128)}, f32[2,768,768]{2,1,0:T(8,128)}, bf16[2,4,32,768]{3,2,1,0:T(8,128)(2,1)}, f32[256,768]{1,0:T(8,128)}, f32[3,19...) custom-call(bf16[2,2,16,16,768]{4,3,2,1,0:T(8,128)(2,1)S(1)} %get-tuple-, ...), custom_call_target="tpu_custom_call" | custom-call | tf_op jit(solution)/shard_map/last_outputs/pallas_call | solution.py:880
